TPU v7x, 512 devices: a whole 4x8x8 slice. The times are simulated.
512 devices in a mesh: row: 16 (over y, core), col: 32 (over z, x).
Axes of the slice: x: 4, y: 8, z: 8, core: 2. Of those that a mesh axis runs over, the one named last changes fastest.
Arguments:
- patches: float32 [512, 6144], P('col', 'row'), may hold values from -6 to 6
- cotangent: float32 [512, 6144], P('col', 'row'), may hold values from -1.5 to 1.5
- expand_weight: float32 [6144, 12288], P('row', 'col'), may hold values from -0.078125 to 0.078125
- reduce_weight: float32 [12288, 6144], P('col', 'row'), may hold values from -0.0546875 to 0.0546875
Outputs:
- mlp_output: float32 [512, 6144], P('col', 'row')
- patch_grad: float32 [512, 6144], P('col', 'row')
- expand_grad: float32 [6144, 12288], P('row', 'col')
- reduce_grad: float32 [12288, 6144], P('col', 'row')
All inputs are finite; a program needn't handle non-finite values.
Results may differ from a plain program's by a relative error of at most 0.00012.
Values sent between devices are 32-bit elements; how exact they have to be, the bound alone decides.
No kernel may reach another device: no remote copies, remote signals or barrier semaphores. Data moves between devices by JAX's collectives and lax.ppermute only.
A program may use at most 64 MiB of HBM per device.

v0:
```python
import math

import jax
import jax.numpy as jnp
from jax import lax
from jax.sharding import PartitionSpec as P

highest = lax.Precision.HIGHEST


def block_product(operand, weight, flipped):
    if flipped:
        return lax.dot_general(
            operand,
            weight,
            (((1,), (1,)), ((), ())),
            precision=highest,
            preferred_element_type=jnp.float32,
        )
    return lax.dot_general(
        operand,
        weight,
        (((1,), (0,)), ((), ())),
        precision=highest,
        preferred_element_type=jnp.float32,
    )


def row_reduce(term_fn, row_count):
    return lax.psum_scatter(
        term_fn(jnp.int32(0), lax.axis_size("row") * row_count),
        "row",
        scatter_dimension=0,
        tiled=True,
    )


def col_reduce(term_fn, row_count):
    return lax.psum_scatter(
        term_fn(jnp.int32(0), lax.axis_size("col") * row_count),
        "col",
        scatter_dimension=0,
        tiled=True,
    )


def row_collect(block):
    return lax.all_gather(block, "row", axis=0, tiled=True)


def shards(patches, cotangent, expand_weight, reduce_weight):
    full_input, full_cotan = (
        lax.all_gather(patches, "col", axis=0, tiled=True),
        lax.all_gather(cotangent, "col", axis=0, tiled=True),
    )
    tokens = full_input.shape[0]
    row_share = tokens // lax.axis_size("row")
    col_share = tokens // lax.axis_size("col")

    def preact_term(offset, amount):
        return block_product(full_input, expand_weight, False)

    def actgrad_term(offset, amount):
        return block_product(full_cotan, reduce_weight, True)

    preact = row_reduce(preact_term, row_share)
    act_cdf = 0.5 * (1.0 + jax.scipy.special.erf(preact / math.sqrt(2.0)))
    activated = preact * act_cdf
    full_active = row_collect(activated)

    def output_term(offset, amount):
        return block_product(full_active, reduce_weight, False)

    mlp_output = col_reduce(output_term, col_share)
    act_grad = row_reduce(actgrad_term, row_share)
    pre_grad = act_grad * (
        act_cdf + preact * jnp.exp(-0.5 * preact * preact) / math.sqrt(2.0 * math.pi)
    )
    full_pregrad = row_collect(pre_grad)

    def input_term(offset, amount):
        return block_product(full_pregrad, expand_weight, True)

    patch_grad = col_reduce(input_term, col_share)
    expand_grad = lax.dot_general(
        full_input,
        full_pregrad,
        (((0,), (0,)), ((), ())),
        precision=highest,
        preferred_element_type=jnp.float32,
    )
    reduce_grad = lax.dot_general(
        full_active,
        full_cotan,
        (((0,), (0,)), ((), ())),
        precision=highest,
        preferred_element_type=jnp.float32,
    )
    return (mlp_output, patch_grad, expand_grad, reduce_grad)


def solution(mesh):
    placed = (P("col", "row"), P("col", "row"), P("row", "col"), P("col", "row"))
    return jax.shard_map(
        shards,
        mesh=mesh,
        in_specs=placed,
        out_specs=(P("col", "row"), P("col", "row"), P("row", "col"), P("col", "row")),
        check_vma=False,
    )
```

profile of v0, /device:TPU:1, one launch (start us, length us, event | category | flops | bytes accessed | tf_op | source)
XLA Modules:
  0.0 648.5 jit_solution(13052936872570216630)
XLA Ops:
  7.2 0.0 copy-start
  7.2 0.0 copy-start.3
  7.2 0.0 reduce-scatter.9.cloned.1.call-start
  7.2 44.7 %all_gather.14 = f32[512,384]{1,0:T(8,128)S(1)} all-gather(f32[16,384]{1,0:T(8,128)} %param.5), channel_id=1, replica_groups=mesh['row'=16,'col'=32] {'col'}, dimensions={0}, use_global_device_ids=true | all-gather | bytes 811008 | tf_op jit(solution)/shard_map/all_gather | solution.py:54
  51.9 0.0 copy-done.3
  51.9 2.5 fusion.8
  54.4 0.0 copy-start.4
  54.4 0.0 reduce-scatter.9.cloned.1.call-update
  54.4 0.0 reduce-scatter.5.cloned.1.call-start
  54.5 0.7 copy-done.4
  55.1 37.7 %all_gather.12 = f32[512,384]{1,0:T(8,128)S(1)} all-gather(f32[16,384]{1,0:T(8,128)S(1)} %copy-done.4), channel_id=1, replica_groups=mesh['row'=16,'col'=32] {'col'}, dimensions={0}, use_global_device_ids=true | all-gather | bytes 811008 | tf_op jit(solution)/shard_map/all_gather | solution.py:53
  92.8 0.0 copy-done
  92.8 2.5 fusion.6
  95.3 0.0 reduce-scatter.5.cloned.1.call-update
  95.3 0.0 reduce-scatter.11.cloned.1.call-start
  95.4 25.8 %reduce-scatter.9.cloned.1.call-done = f32[32,384]{1,0:T(8,128)} async-done(((f32[512,384]{1,0:T(8,128)}), f32[32,384]{1,0:T(8,128)}) %reduce-scatter.9.cloned.1.call-update) | async-done | bytes 49168 | tf_op jit(solution)/shard_map/reduce_scatter | solution.py:30
  121.2 61.2 %reduce-scatter.5.cloned.1.call-done = f32[32,384]{1,0:T(8,128)} async-done(((f32[512,384]{1,0:T(8,128)}), f32[32,384]{1,0:T(8,128)}) %reduce-scatter.5.cloned.1.call-update) | async-done | bytes 49168 | tf_op jit(solution)/shard_map/reduce_scatter | solution.py:30
  182.5 1.5 fusion.4
  183.9 18.8 %all_gather.15 = f32[512,384]{1,0:T(8,128)S(1)} all-gather(f32[32,384]{1,0:T(8,128)S(1)} %get-tuple-element.8), channel_id=1, replica_groups=mesh['row'=16,'col'=32] {'row'}, dimensions={0}, use_global_device_ids=true | all-gather | bytes 835584 | tf_op jit(solution)/shard_map/all_gather | solution.py:48
  202.8 2.5 fusion.9
  205.3 0.0 reduce-scatter.11.cloned.1.call-update
  205.3 0.0 reduce-scatter.7.cloned.1.call-start
  205.4 18.2 %all_gather.13 = f32[512,384]{1,0:T(8,128)S(1)} all-gather(f32[32,384]{1,0:T(8,128)} %get-tuple-element.9), channel_id=1, replica_groups=mesh['row'=16,'col'=32] {'row'}, dimensions={0}, use_global_device_ids=true | all-gather | bytes 835584 | tf_op jit(solution)/shard_map/all_gather | solution.py:48
  223.5 0.0 copy-start.1
  223.5 0.9 copy-done.1
  224.4 2.5 fusion.7
  226.9 0.0 reduce-scatter.7.cloned.1.call-update
  227.0 1.4 convolution_bitcast_fusion
  228.4 0.0 copy-start.2
  228.4 1.1 copy.8
  229.5 0.1 copy-done.2
  229.5 2.3 fusion.10
  231.8 187.4 %reduce-scatter.11.cloned.1.call-done = f32[16,384]{1,0:T(8,128)} async-done(((f32[512,384]{1,0:T(8,128)}), f32[16,384]{1,0:T(8,128)}) %reduce-scatter.11.cloned.1.call-update) | async-done | bytes 24592 | tf_op jit(solution)/shard_map/reduce_scatter | solution.py:39
  419.2 222.7 %reduce-scatter.7.cloned.1.call-done = f32[16,384]{1,0:T(8,128)} async-done(((f32[512,384]{1,0:T(8,128)}), f32[16,384]{1,0:T(8,128)}) %reduce-scatter.7.cloned.1.call-update) | async-done | bytes 24592 | tf_op jit(solution)/shard_map/reduce_scatter | solution.py:39
Async XLA Ops:
  7.2 85.6 %copy-start = (f32[384,384]{1,0:T(8,128)S(1)}, f32[384,384]{1,0:T(8,128)}, u32[]{:S(2)}) copy-start(f32[384,384]{1,0:T(8,128)} %param.6) | copy-start | bytes 1769476
  7.2 44.7 %copy-start.3 = (f32[384,384]{1,0:T(8,128)S(1)}, f32[384,384]{1,0:T(8,128)}, u32[]{:S(2)}) copy-start(f32[384,384]{1,0:T(8,128)} %param.7) | copy-start | bytes 1769476
  7.2 114.0 %reduce-scatter.9.cloned.1.call-start = ((), (), s32[]{:S(2)}) async-start(), calls=%async_computation.6 | async-start | bytes 835584 | tf_op jit(solution)/shard_map/reduce_scatter | solution.py:30
  54.4 0.7 copy-start.4
  54.4 128.0 %reduce-scatter.5.cloned.1.call-start = ((), (), s32[]{:S(2)}) async-start(), calls=%async_computation.4 | async-start | bytes 835584 | tf_op jit(solution)/shard_map/reduce_scatter | solution.py:30
  95.3 323.8 %reduce-scatter.11.cloned.1.call-start = ((), (), s32[]{:S(2)}) async-start(), calls=%async_computation.7 | async-start | bytes 811008 | tf_op jit(solution)/shard_map/reduce_scatter | solution.py:39
  205.3 436.6 %reduce-scatter.7.cloned.1.call-start = ((), (), s32[]{:S(2)}) async-start(), calls=%async_computation.5 | async-start | bytes 811008 | tf_op jit(solution)/shard_map/reduce_scatter | solution.py:39
  223.5 0.9 copy-start.1
  228.4 1.1 copy-start.2
Sparse Core Ops, SparseCore 0:
  54.5 66.6 reduce-scatter.8
  124.3 58.1 reduce-scatter.4
  205.4 213.7 reduce-scatter.10
  424.0 217.8 reduce-scatter.6
where the time goes:
time: 653 us; the launch traced here: 648 us
  waiting for transfers between devices  497 us (76%)
  blocking collectives  119 us (18%)
  between operations  13.8 us (2%)
  matrix products  13.7 us (2%)
    reduce_scatter x2, waiting for transfers between devices, col_reduce(): lax.psum_scatter(term_fn(jnp.int32(0), lax.axis_size('col') * row_count),...  410 us
    reduce_scatter x2, waiting for transfers between devices, row_reduce(): lax.psum_scatter(term_fn(jnp.int32(0), lax.axis_size('row') * row_count),...  87.1 us
    all_gather x1, blocking collectives, shards(): lax.all_gather(cotangent, 'col', axis=0, tiled=True)  44.7 us
    all_gather x1, blocking collectives, shards(): lax.all_gather(patches, 'col', axis=0, tiled=True)  37.7 us
    all_gather x2, blocking collectives, row_collect(): return lax.all_gather(block, 'row', axis=0, tiled=True)  37 us
  transfers between devices with their start and end apart: 4, of which 4 were waited for; matrix products, arithmetic and copies ran while one was open for 2% of the time, Pallas kernels for 0%

commit v1 on v0

v1 whole, which is shorter than its diff:
```python
import math

import jax
import jax.numpy as jnp
from jax import lax
from jax.sharding import Mesh, PartitionSpec as P

precise = lax.Precision.HIGH
Y, CORE, Z, X = 8, 2, 8, 4


def product(left, right, dims):
    return lax.dot_general(
        left, right, (dims, ((), ())), precision=precise, preferred_element_type=jnp.float32
    )


def from_x(block, step):
    return lax.ppermute(block, "x", [((i + step) % X, i) for i in range(X)])


def to_x(block, step):
    return lax.ppermute(block, "x", [(i, (i + step) % X) for i in range(X)])


def swap_cores(block):
    return lax.ppermute(block, "core", [(0, 1), (1, 0)])


def everyone(block, axis, size):
    copies = jnp.broadcast_to(block[None], (size, *block.shape))
    return lax.all_to_all(copies, axis, split_axis=0, concat_axis=0, tiled=True)


def own_half_first(block, core):
    half = block.shape[0] // 2
    first, second = block[:half], block[half:]
    return jnp.stack(
        [jnp.where(core == 0, first, second), jnp.where(core == 0, second, first)]
    )


def shards(patches, cotangent, expand_weight, reduce_weight):
    core = lax.axis_index("core")
    width = patches.shape[1]
    hidden = expand_weight.shape[1]
    tokens = patches.shape[0]
    half = tokens // 2

    mine = own_half_first(jnp.concatenate([patches, cotangent], axis=1), core)
    over_z = everyone(mine, "z", Z)
    over_z = over_z.transpose(1, 0, 2, 3).reshape(2, Z * half, 2 * width)
    pieces = [over_z] + [from_x(over_z, k) for k in (1, 2, 3)]
    gathered = jnp.stack(pieces, axis=1)
    gathered = gathered.reshape(2, X * Z * half, 2 * width)
    full_in, full_cot = gathered[..., :width], gathered[..., width:]

    def terms(part):
        return jnp.concatenate(
            [
                product(full_in[part], expand_weight, ((1,), (0,))),
                product(full_cot[part], reduce_weight, ((1,), (1,))),
            ],
            axis=1,
        )

    away = swap_cores(terms(1))
    summed = terms(0) + away
    share = summed.shape[0] // Y
    parts = lax.all_to_all(
        summed.reshape(Y, share, 2 * hidden), "y", split_axis=0, concat_axis=0, tiled=True
    )
    total = jnp.sum(parts, axis=0)
    preact, act_grad = total[:, :hidden], total[:, hidden:]
    act_cdf = 0.5 * (1.0 + jax.scipy.special.erf(preact / math.sqrt(2.0)))
    activated = preact * act_cdf
    pre_grad = act_grad * (
        act_cdf + preact * jnp.exp(-0.5 * preact * preact) / math.sqrt(2.0 * math.pi)
    )
    near = everyone(jnp.concatenate([activated, pre_grad], axis=1), "y", Y)
    near = near.reshape(Y * share, 2 * hidden)
    far = swap_cores(near)
    both = jnp.stack([near, far])

    def results(part):
        return jnp.concatenate(
            [
                product(part[:, :hidden], reduce_weight, ((1,), (0,))),
                product(part[:, hidden:], expand_weight, ((1,), (1,))),
            ],
            axis=1,
        )

    outs = jnp.stack([results(near), results(far)]).reshape(2, X, Z, half, 2 * width)
    outs = outs.transpose(1, 2, 0, 3, 4)
    summed = outs[0]
    arrived = [to_x(outs[k], k) for k in (1, 2, 3)]
    summed = summed + arrived[0] + arrived[1] + arrived[2]
    last = jnp.sum(
        lax.all_to_all(summed, "z", split_axis=0, concat_axis=0, tiled=True), axis=0
    )
    last = own_half_first(last.reshape(tokens, 2 * width), core).reshape(tokens, 2 * width)

    flat = both.reshape(-1, 2 * hidden)
    all_in = full_in.reshape(-1, width)
    all_cot = full_cot.reshape(-1, width)
    expand_grad = product(all_in, flat[:, hidden:], ((0,), (0,)))
    reduce_grad = product(flat[:, :hidden], all_cot, ((0,), (0,)))
    return last[:, :width], last[:, width:], expand_grad, reduce_grad


def solution(mesh):
    fine = Mesh(mesh.devices.reshape(Y, CORE, Z, X), ("y", "core", "z", "x"))
    row, col = ("y", "core"), ("z", "x")
    placed = (P(col, row), P(col, row), P(row, col), P(col, row))
    return jax.shard_map(
        shards, mesh=fine, in_specs=placed, out_specs=placed, check_vma=False
    )
```

time: 653 us -> 162 us (0.25)
  the two profiles are of different devices: /device:TPU:1 before, /device:TPU:2 now
where the time goes in v1:
time: 162 us; the launch traced here: 161 us
  blocking collectives  79.8 us (49%)
  waiting for transfers between devices  37.1 us (23%)
  starting transfers between devices  27 us (17%)
  matrix products  7.56 us (5%)
  local copies, waits for them, and re-layouts  4.73 us (3%)
  other arithmetic  4.2 us (3%)
    all_to_all x2, blocking collectives, everyone(): return lax.all_to_all(copies, axis, split_axis=0, concat_axis=0, tiled=True)  49.5 us
    all_to_all x1, blocking collectives, shards(): lax.all_to_all(summed.reshape(Y, share, 2 * hidden), 'y', split_axis=0, c...  30.3 us
    ppermute x3, waiting for transfers between devices, to_x(): return lax.ppermute(block, 'x', [(i, (i + step) % X) for i in range(X)])  14.1 us
    ppermute x3, waiting for transfers between devices, from_x(): return lax.ppermute(block, 'x', [((i + step) % X, i) for i in range(X)])  11.4 us
    ppermute x3, starting transfers between devices, from_x(): return lax.ppermute(block, 'x', [((i + step) % X, i) for i in range(X)])  9.88 us
    ppermute x3, starting transfers between devices, to_x(): return lax.ppermute(block, 'x', [(i, (i + step) % X) for i in range(X)])  9.85 us
    all_to_all x1, waiting for transfers between devices, shards(): lax.all_to_all(summed, 'z', split_axis=0, concat_axis=0, tiled=True)  9.4 us
    dot_general x10, matrix products, product(): lax.dot_general(left, right, (dims, ((), ())), precision=precise, preferr...  7.56 us
  transfers between devices with their start and end apart: 9, of which 8 were waited for; matrix products, arithmetic and copies ran while one was open for 5% of the time, Pallas kernels for 0%

profile of v1, /device:TPU:2, one launch (start us, length us, event | category | flops | bytes accessed | tf_op | source)
XLA Modules:
  0.0 161.4 jit_solution(1166085942220510243)
XLA Ops:
  0.6 0.8 constant_dynamic-update-slice_fusion.1
  1.5 0.7 constant_dynamic-update-slice_fusion
  2.2 24.8 %all_to_all.20 = f32[8,2,8,768]{3,2,1,0:T(8,128)S(1)} all-to-all(f32[8,2,8,768]{3,2,1,0:T(8,128)S(1)} %broadcast_in_dim.4), channel_id=1, replica_groups=mesh['y'=8,'core'=2,'z'=8,'x'=4] {'z'}, dimensions={0} | all-to-all | bytes 786432 | tf_op jit(solution)/shard_map/all_to_all | solution.py:32
  27.1 4.0 %collective-permute-start.1 = (f32[2,64,768]{2,1,0:T(8,128)S(1)}, f32[2,64,768]{2,1,0:T(8,128)S(1)}, u32[]{:S(2)}, u32[]{:S(2)}) collective-permute-start(f32[2,64,768]{2,1,0:T(8,128)S(1)} %bitcast.86), channel_id=1, source_target_pairs={{2,0},{3,1},{0,2},{1,3},{6,4},{7,5},{4,6},{5,7},{10,8},{11,9},{8,1... | collective-permute-start | bytes 1179656 | tf_op jit(solution)/shard_map/ppermute | solution.py:19
  31.1 3.3 %collective-permute-start = (f32[2,64,768]{2,1,0:T(8,128)S(1)}, f32[2,64,768]{2,1,0:T(8,128)S(1)}, u32[]{:S(2)}, u32[]{:S(2)}) collective-permute-start(f32[2,64,768]{2,1,0:T(8,128)S(1)} %bitcast.87), channel_id=1, source_target_pairs={{1,0},{2,1},{3,2},{0,3},{5,4},{6,5},{7,6},{4,7},{9,8},{10,9},{11,1... | collective-permute-start | bytes 1179656 | tf_op jit(solution)/shard_map/ppermute | solution.py:19
  34.5 2.5 %collective-permute-start.2 = (f32[2,64,768]{2,1,0:T(8,128)S(1)}, f32[2,64,768]{2,1,0:T(8,128)S(1)}, u32[]{:S(2)}, u32[]{:S(2)}) collective-permute-start(f32[2,64,768]{2,1,0:T(8,128)S(1)} %bitcast.88), channel_id=1, source_target_pairs={{3,0},{0,1},{1,2},{2,3},{7,4},{4,5},{5,6},{6,7},{11,8},{8,9},{9,10... | collective-permute-start | bytes 1179656 | tf_op jit(solution)/shard_map/ppermute | solution.py:19
  37.0 5.6 %collective-permute-done.1 = f32[2,64,768]{2,1,0:T(8,128)S(1)} collective-permute-done((f32[2,64,768]{2,1,0:T(8,128)S(1)}, f32[2,64,768]{2,1,0:T(8,128)S(1)}, u32[]{:S(2)}, u32[]{:S(2)}) %collective-permute-start.1) | collective-permute-done | bytes 393248 | tf_op jit(solution)/shard_map/ppermute | solution.py:19
  42.6 5.7 %collective-permute-done = f32[2,64,768]{2,1,0:T(8,128)S(1)} collective-permute-done((f32[2,64,768]{2,1,0:T(8,128)S(1)}, f32[2,64,768]{2,1,0:T(8,128)S(1)}, u32[]{:S(2)}, u32[]{:S(2)}) %collective-permute-start) | collective-permute-done | bytes 393248 | tf_op jit(solution)/shard_map/ppermute | solution.py:19
  48.3 0.1 pad_maximum_fusion
  48.5 0.1 copy.21
  48.6 0.9 copy-done.1
  49.5 0.5 fusion.15
  50.1 0.5 fusion.16
  50.6 0.1 pad_maximum_fusion.2
  50.7 1.9 %collective-permute-start.3 = (f32[256,768]{1,0:T(8,128)S(1)}, f32[256,768]{1,0:T(8,128)S(1)}, u32[]{:S(2)}, u32[]{:S(2)}) collective-permute-start(f32[256,768]{1,0:T(8,128)S(1)} %pad_maximum_fusion.2), channel_id=1, source_target_pairs={{0,32},{32,0},{1,33},{33,1},{2,34},{34,2},{3,35},{35,3},{4,36},{36... | collective-permute-start | bytes 2359304 | tf_op jit(solution)/shard_map/ppermute | solution.py:27
  52.6 0.5 fusion.17
  53.2 0.5 fusion.18
  53.7 1.2 collective-permute-done.3
  54.9 0.1 maximum_add_fusion
  54.9 30.3 %all_to_all.21 = f32[8,32,768]{2,1,0:T(8,128)S(1)} all-to-all(f32[8,32,768]{2,1,0:T(8,128)S(1)} %bitcast.83), channel_id=1, replica_groups=mesh['y'=8,'core'=2,'z'=8,'x'=4] {'y'}, dimensions={0} | all-to-all | bytes 1572864 | tf_op jit(solution)/shard_map/all_to_all | solution.py:70
  85.3 0.7 reduce_sum.18
  85.9 0.9 slice_multiply_fusion
  86.8 0.1 broadcast_in_dim.5
  86.9 24.7 %all_to_all.22 = f32[8,32,768]{2,1,0:T(8,128)S(1)} all-to-all(f32[8,32,768]{2,1,0:T(8,128)S(1)} %broadcast_in_dim.5), channel_id=1, replica_groups=mesh['y'=8,'core'=2,'z'=8,'x'=4] {'y'}, dimensions={0} | all-to-all | bytes 1572864 | tf_op jit(solution)/shard_map/all_to_all | solution.py:32
  111.6 1.9 %collective-permute-start.4 = (f32[256,768]{1,0:T(8,128)S(1)}, f32[256,768]{1,0:T(8,128)S(1)}, u32[]{:S(2)}, u32[]{:S(2)}) collective-permute-start(f32[256,768]{1,0:T(8,128)S(1)} %bitcast.74), channel_id=1, source_target_pairs={{0,32},{32,0},{1,33},{33,1},{2,34},{34,2},{3,35},{35,3},{4,36},{36... | collective-permute-start | bytes 2359304 | tf_op jit(solution)/shard_map/ppermute | solution.py:27
  113.5 0.5 fusion.11
  114.1 0.5 fusion.13
  114.6 0.1 pad_maximum_fusion.3
  114.7 1.1 collective-permute-done.4
  115.8 0.5 fusion.7
  116.3 0.5 fusion.9
  116.9 0.1 pad_maximum_fusion.4
  116.9 0.1 maximum_bitcast_fusion
  117.1 0.1 slice_bitcast_fusion.2
  117.2 3.4 %collective-permute-start.5 = (f32[8,2,8,768]{3,2,1,0:T(8,128)S(1)}, f32[8,2,8,768]{3,2,1,0:T(8,128)S(1)}, u32[]{:S(2)}, u32[]{:S(2)}) collective-permute-start(f32[8,2,8,768]{3,2,1,0:T(8,128)S(1)} %get-tuple-element.6), channel_id=1, source_target_pairs={{0,1},{1,2},{2,3},{3,0},{4,5},{5,6},{6,7},{7,4},{8,9},{9,10},{10,1... | collective-permute-start | bytes 1179656 | tf_op jit(solution)/shard_map/ppermute | solution.py:23
  120.5 2.5 %collective-permute-start.7 = (f32[8,2,8,768]{3,2,1,0:T(8,128)S(1)}, f32[8,2,8,768]{3,2,1,0:T(8,128)S(1)}, u32[]{:S(2)}, u32[]{:S(2)}) collective-permute-start(f32[8,2,8,768]{3,2,1,0:T(8,128)S(1)} %get-tuple-element.7), channel_id=1, source_target_pairs={{0,3},{1,0},{2,1},{3,2},{4,7},{5,4},{6,5},{7,6},{8,11},{9,8},{10,9... | collective-permute-start | bytes 1179656 | tf_op jit(solution)/shard_map/ppermute | solution.py:23
  123.0 4.0 %collective-permute-start.6 = (f32[8,2,8,768]{3,2,1,0:T(8,128)S(1)}, f32[8,2,8,768]{3,2,1,0:T(8,128)S(1)}, u32[]{:S(2)}, u32[]{:S(2)}) collective-permute-start(f32[8,2,8,768]{3,2,1,0:T(8,128)S(1)} %get-tuple-element.8), channel_id=1, source_target_pairs={{0,2},{1,3},{2,0},{3,1},{4,6},{5,7},{6,4},{7,5},{8,10},{9,11},{10,... | collective-permute-start | bytes 1179656 | tf_op jit(solution)/shard_map/ppermute | solution.py:23
  127.0 1.3 fusion.24
  128.3 2.7 %collective-permute-done.5 = f32[8,2,8,768]{3,2,1,0:T(8,128)S(1)} collective-permute-done((f32[8,2,8,768]{3,2,1,0:T(8,128)S(1)}, f32[8,2,8,768]{3,2,1,0:T(8,128)S(1)}, u32[]{:S(2)}, u32[]{:S(2)}) %collective-permute-start.5) | collective-permute-done | bytes 393248 | tf_op jit(solution)/shard_map/ppermute | solution.py:23
  131.0 2.8 %collective-permute-done.7 = f32[8,2,8,768]{3,2,1,0:T(8,128)S(1)} collective-permute-done((f32[8,2,8,768]{3,2,1,0:T(8,128)S(1)}, f32[8,2,8,768]{3,2,1,0:T(8,128)S(1)}, u32[]{:S(2)}, u32[]{:S(2)}) %collective-permute-start.7) | collective-permute-done | bytes 393248 | tf_op jit(solution)/shard_map/ppermute | solution.py:23
  133.8 8.6 %collective-permute-done.6 = f32[8,2,8,768]{3,2,1,0:T(8,128)S(1)} collective-permute-done((f32[8,2,8,768]{3,2,1,0:T(8,128)S(1)}, f32[8,2,8,768]{3,2,1,0:T(8,128)S(1)}, u32[]{:S(2)}, u32[]{:S(2)}) %collective-permute-start.6) | collective-permute-done | bytes 393248 | tf_op jit(solution)/shard_map/ppermute | solution.py:23
  142.4 0.8 fusion.6
  143.2 3.5 %all-to-all-start.3 = ((f32[8,2,8,768]{3,2,1,0:T(8,128)}), f32[8,2,8,768]{3,2,1,0:T(8,128)S(1)}, u32[]{:S(2)}, u32[]{:S(2)}) async-start(f32[8,2,8,768]{3,2,1,0:T(8,128)} %fusion.6), calls=%async_computation.3 | async-start | bytes 786432 | tf_op jit(solution)/shard_map/all_to_all | solution.py:100
  146.7 1.3 pad_maximum_fusion.1
  148.0 1.6 %fusion = f32[384,384]{1,0:T(8,128)} fusion(f32[512,384]{1,0:T(8,128)S(1)} %bitcast.81, f32[512,768]{1,0:T(8,128)S(1)} %bitcast.78), kind=kOutput, calls=%fused_computation.3 | convolution fusion | flops 452984832 | bytes 2162688 | tf_op jit(solution)/shard_map/dot_general | solution.py:13
  149.7 1.6 %fusion.2 = f32[384,384]{1,0:T(8,128)} fusion(f32[512,384]{1,0:T(8,128)S(1)} %bitcast.80, f32[512,768]{1,0:T(8,128)S(1)} %bitcast.79), kind=kOutput, calls=%fused_computation.5 | convolution fusion | flops 452984832 | bytes 2162688 | tf_op jit(solution)/shard_map/dot_general | solution.py:13
  151.3 9.4 %all-to-all-done.3 = f32[8,2,8,768]{3,2,1,0:T(8,128)S(1)} async-done(((f32[8,2,8,768]{3,2,1,0:T(8,128)}), f32[8,2,8,768]{3,2,1,0:T(8,128)S(1)}, u32[]{:S(2)}, u32[]{:S(2)}) %all-to-all-start.3) | async-done | bytes 393248 | tf_op jit(solution)/shard_map/all_to_all | solution.py:100
  160.7 0.6 fusion.25
  (18 shorter events, 0.2 us)
Async XLA Ops:
  0.6 49.4 %copy-start = (f32[384,384]{1,0:T(8,128)S(1)}, f32[384,384]{1,0:T(8,128)}, u32[]{:S(2)}) copy-start(f32[384,384]{1,0:T(8,128)} %param.6) | copy-start | bytes 1769476
  27.1 15.5 %collective-permute-start.1 = (f32[2,64,768]{2,1,0:T(8,128)S(1)}, f32[2,64,768]{2,1,0:T(8,128)S(1)}, u32[]{:S(2)}, u32[]{:S(2)}) collective-permute-start(f32[2,64,768]{2,1,0:T(8,128)S(1)} %bitcast.86), channel_id=1, source_target_pairs={{2,0},{3,1},{0,2},{1,3},{6,4},{7,5},{4,6},{5,7},{10,8},{11,9},{8,1... | collective-permute-start | bytes 1179656 | tf_op jit(solution)/shard_map/ppermute | solution.py:19
  31.1 17.2 %collective-permute-start = (f32[2,64,768]{2,1,0:T(8,128)S(1)}, f32[2,64,768]{2,1,0:T(8,128)S(1)}, u32[]{:S(2)}, u32[]{:S(2)}) collective-permute-start(f32[2,64,768]{2,1,0:T(8,128)S(1)} %bitcast.87), channel_id=1, source_target_pairs={{1,0},{2,1},{3,2},{0,3},{5,4},{6,5},{7,6},{4,7},{9,8},{10,9},{11,1... | collective-permute-start | bytes 1179656 | tf_op jit(solution)/shard_map/ppermute | solution.py:19
  34.5 13.9 %collective-permute-start.2 = (f32[2,64,768]{2,1,0:T(8,128)S(1)}, f32[2,64,768]{2,1,0:T(8,128)S(1)}, u32[]{:S(2)}, u32[]{:S(2)}) collective-permute-start(f32[2,64,768]{2,1,0:T(8,128)S(1)} %bitcast.88), channel_id=1, source_target_pairs={{3,0},{0,1},{1,2},{2,3},{7,4},{4,5},{5,6},{6,7},{11,8},{8,9},{9,10... | collective-permute-start | bytes 1179656 | tf_op jit(solution)/shard_map/ppermute | solution.py:19
  48.5 1.1 copy-start.1
  50.7 4.2 %collective-permute-start.3 = (f32[256,768]{1,0:T(8,128)S(1)}, f32[256,768]{1,0:T(8,128)S(1)}, u32[]{:S(2)}, u32[]{:S(2)}) collective-permute-start(f32[256,768]{1,0:T(8,128)S(1)} %pad_maximum_fusion.2), channel_id=1, source_target_pairs={{0,32},{32,0},{1,33},{33,1},{2,34},{34,2},{3,35},{35,3},{4,36},{36... | collective-permute-start | bytes 2359304 | tf_op jit(solution)/shard_map/ppermute | solution.py:27
  111.6 4.2 %collective-permute-start.4 = (f32[256,768]{1,0:T(8,128)S(1)}, f32[256,768]{1,0:T(8,128)S(1)}, u32[]{:S(2)}, u32[]{:S(2)}) collective-permute-start(f32[256,768]{1,0:T(8,128)S(1)} %bitcast.74), channel_id=1, source_target_pairs={{0,32},{32,0},{1,33},{33,1},{2,34},{34,2},{3,35},{35,3},{4,36},{36... | collective-permute-start | bytes 2359304 | tf_op jit(solution)/shard_map/ppermute | solution.py:27
  115.8 1.2 copy-start.4
  117.2 13.9 %collective-permute-start.5 = (f32[8,2,8,768]{3,2,1,0:T(8,128)S(1)}, f32[8,2,8,768]{3,2,1,0:T(8,128)S(1)}, u32[]{:S(2)}, u32[]{:S(2)}) collective-permute-start(f32[8,2,8,768]{3,2,1,0:T(8,128)S(1)} %get-tuple-element.6), channel_id=1, source_target_pairs={{0,1},{1,2},{2,3},{3,0},{4,5},{5,6},{6,7},{7,4},{8,9},{9,10},{10,1... | collective-permute-start | bytes 1179656 | tf_op jit(solution)/shard_map/ppermute | solution.py:23
  120.5 13.3 %collective-permute-start.7 = (f32[8,2,8,768]{3,2,1,0:T(8,128)S(1)}, f32[8,2,8,768]{3,2,1,0:T(8,128)S(1)}, u32[]{:S(2)}, u32[]{:S(2)}) collective-permute-start(f32[8,2,8,768]{3,2,1,0:T(8,128)S(1)} %get-tuple-element.7), channel_id=1, source_target_pairs={{0,3},{1,0},{2,1},{3,2},{4,7},{5,4},{6,5},{7,6},{8,11},{9,8},{10,9... | collective-permute-start | bytes 1179656 | tf_op jit(solution)/shard_map/ppermute | solution.py:23
  123.0 19.4 %collective-permute-start.6 = (f32[8,2,8,768]{3,2,1,0:T(8,128)S(1)}, f32[8,2,8,768]{3,2,1,0:T(8,128)S(1)}, u32[]{:S(2)}, u32[]{:S(2)}) collective-permute-start(f32[8,2,8,768]{3,2,1,0:T(8,128)S(1)} %get-tuple-element.8), channel_id=1, source_target_pairs={{0,2},{1,3},{2,0},{3,1},{4,6},{5,7},{6,4},{7,5},{8,10},{9,11},{10,... | collective-permute-start | bytes 1179656 | tf_op jit(solution)/shard_map/ppermute | solution.py:23
  143.2 17.5 %all-to-all-start.3 = ((f32[8,2,8,768]{3,2,1,0:T(8,128)}), f32[8,2,8,768]{3,2,1,0:T(8,128)S(1)}, u32[]{:S(2)}, u32[]{:S(2)}) async-start(f32[8,2,8,768]{3,2,1,0:T(8,128)} %fusion.6), calls=%async_computation.3 | async-start | bytes 786432 | tf_op jit(solution)/shard_map/all_to_all | solution.py:100
  146.7 1.4 copy-start.3
  148.0 1.7 %copy-start.2 = (f32[2,256,384]{2,1,0:T(8,128)S(1)}, f32[2,256,384]{2,1,0:T(8,128)}, u32[]{:S(2)}) copy-start(f32[2,256,384]{2,1,0:T(8,128)} %get-tuple-element.5) | copy-start | bytes 2359300

commit v2 on v1

v2 whole, which is shorter than its diff:
```python
import math

import jax
import jax.numpy as jnp
from jax import lax
from jax.sharding import Mesh, PartitionSpec as P

precise = lax.Precision.HIGH
Y, CORE, ZH, ZL, XH, XL = 8, 2, 4, 2, 2, 2
N_FAR, N_NEAR = ZH * XH, ZL * XL
Z, X = ZH * ZL, XH * XL
FAR = ("zh", "xh", "core")
CELL = ("core", "zh", "zl", "xh", "xl")
BLOCKS = [
    [
        (c * Z + (z + (p + c) % 2 + c) % Z) * X + (x + (q + c) % 2 + c) % X
        for p in range(2)
        for q in range(2)
    ]
    for c in range(CORE)
    for z in range(0, Z, 2)
    for x in range(0, X, 2)
]


def product(left, right, dims):
    return lax.dot_general(
        left, right, (dims, ((), ())), precision=precise, preferred_element_type=jnp.float32
    )


def swap_cores(block):
    return lax.ppermute(block, "core", [(0, 1), (1, 0)])


def exchange(blocks, axis, groups=None):
    return lax.all_to_all(
        blocks, axis, split_axis=0, concat_axis=0, tiled=True, axis_index_groups=groups
    )


def copies(block, count):
    return jnp.broadcast_to(block[None], (count, *block.shape))


def shards(patches, cotangent, expand_weight, reduce_weight):
    core = lax.axis_index("core")
    tokens, width = patches.shape
    hidden = expand_weight.shape[1]
    part = tokens // CORE

    def in_order(own, other):
        return jnp.where(core == 0, own, other), jnp.where(core == 0, other, own)

    mine = jnp.stack(
        [patches.reshape(CORE, part, width), cotangent.reshape(CORE, part, width)], axis=1
    )
    far = exchange(copies(mine, N_FAR).reshape(N_FAR * CORE, 2, part, width), FAR)
    far = far.reshape(N_FAR, CORE, 2, part, width).transpose(1, 2, 0, 3, 4)
    far = far.reshape(CORE, 2, N_FAR * part, width)
    inputs = exchange(copies(far, N_NEAR), CELL, BLOCKS)
    rows = N_NEAR * N_FAR * part

    others = swap_cores(jnp.stack([expand_weight, reduce_weight]))
    expand = in_order(expand_weight, others[0])
    reduce = in_order(reduce_weight, others[1])

    full_in = [inputs[:, c, 0].reshape(rows, width) for c in range(CORE)]
    full_cot = [inputs[:, c, 1].reshape(rows, width) for c in range(CORE)]
    terms = jnp.stack(
        [
            product(full_in[0], expand[0], ((1,), (0,)))
            + product(full_in[1], expand[1], ((1,), (0,))),
            product(full_cot[0], reduce[0], ((1,), (1,)))
            + product(full_cot[1], reduce[1], ((1,), (1,))),
        ]
    )
    share = rows // Y
    terms = terms.reshape(2, Y, share, hidden).transpose(1, 0, 2, 3)
    preact, act_grad = jnp.sum(exchange(terms, "y"), axis=0)
    act_cdf = 0.5 * (1.0 + jax.scipy.special.erf(preact / math.sqrt(2.0)))
    activated = preact * act_cdf
    pre_grad = act_grad * (
        act_cdf + preact * jnp.exp(-0.5 * preact * preact) / math.sqrt(2.0 * math.pi)
    )
    both = exchange(copies(jnp.stack([activated, pre_grad]), Y), "y")
    full_active, full_pregrad = (both[:, k].reshape(rows, hidden) for k in range(2))

    outs = jnp.stack(
        [
            jnp.stack(
                [
                    product(full_active, reduce[c], ((1,), (0,))),
                    product(full_pregrad, expand[c], ((1,), (1,))),
                ]
            )
            for c in range(CORE)
        ]
    )
    outs = outs.reshape(CORE, 2, N_NEAR, N_FAR * part, width).transpose(2, 0, 1, 3, 4)
    outs, full_active, full_pregrad = lax.optimization_barrier((outs, full_active, full_pregrad))
    near = jnp.sum(exchange(outs, CELL, BLOCKS), axis=0)
    near = near.reshape(CORE, 2, N_FAR, part, width).transpose(2, 0, 1, 3, 4)
    last = exchange(near.reshape(N_FAR * CORE, 2, part, width), FAR)
    last = jnp.sum(last.reshape(N_FAR, CORE, 2, part, width), axis=0)
    mlp_output, patch_grad = (last[:, k].reshape(tokens, width) for k in range(2))

    grads = [
        (
            product(full_in[c], full_pregrad, ((0,), (0,))),
            product(full_active, full_cot[c], ((0,), (0,))),
        )
        for c in range(CORE)
    ]
    own, away = zip(*[in_order(a, b) for a, b in zip(*grads)])
    away = swap_cores(jnp.stack(away))
    return mlp_output, patch_grad, own[0] + away[0], own[1] + away[1]


def solution(mesh):
    fine = Mesh(
        mesh.devices.reshape(Y, CORE, ZH, ZL, XH, XL), ("y", "core", "zh", "zl", "xh", "xl")
    )
    row, col = ("y", "core"), ("zh", "zl", "xh", "xl")
    placed = (P(col, row), P(col, row), P(row, col), P(col, row))
    return jax.shard_map(
        shards, mesh=fine, in_specs=placed, out_specs=placed, check_vma=False
    )
```

time: 162 us -> 152 us (0.938)
  the two profiles are of different devices: /device:TPU:2 before, /device:TPU:1 now
where the time goes in v2:
time: 152 us; the launch traced here: 150 us
  blocking collectives  79.4 us (52%)
  waiting for transfers between devices  26.4 us (17%)
  starting transfers between devices  22.1 us (15%)
  matrix products  7.46 us (5%)
  other arithmetic  7.11 us (5%)
  local copies, waits for them, and re-layouts  6.33 us (4%)
    all_to_all x3, blocking collectives, exchange(): lax.all_to_all(blocks, axis, split_axis=0, concat_axis=0, tiled=True, axi...  79.4 us
    all_to_all x3, waiting for transfers between devices, exchange(): lax.all_to_all(blocks, axis, split_axis=0, concat_axis=0, tiled=True, axi...  26.4 us
    all_to_all x3, starting transfers between devices, exchange(): lax.all_to_all(blocks, axis, split_axis=0, concat_axis=0, tiled=True, axi...  18.2 us
    dot_general x12, matrix products, product(): lax.dot_general(left, right, (dims, ((), ())), precision=precise, preferr...  7.46 us
    ppermute x2, starting transfers between devices, swap_cores(): return lax.ppermute(block, 'core', [(0, 1), (1, 0)])  3.82 us
  transfers between devices with their start and end apart: 5, of which 3 were waited for; matrix products, arithmetic and copies ran while one was open for 7% of the time, Pallas kernels for 0%

profile of v2, /device:TPU:1, one launch (start us, length us, event | category | flops | bytes accessed | tf_op | source)
XLA Modules:
  0.0 149.8 jit_solution(6995607801262321064)
XLA Ops:
  0.6 0.8 pad_maximum_fusion.3
  1.4 27.8 %all_to_all.30 = f32[16,2,8,384]{3,2,1,0:T(8,128)S(1)} all-to-all(f32[16,2,8,384]{3,2,1,0:T(8,128)S(1)} %bitcast.135), channel_id=1, replica_groups=mesh['y'=8,'core'=2,'zh'=4,'zl'=2,'xh'=2,'xl'=2] {'zh','xh','core'}, dimensions={0} | all-to-all | bytes 786432 | tf_op jit(solution)/shard_map/all_to_all | solution.py:37
  29.3 1.3 broadcast_in_dim.10
  30.6 5.5 %all-to-all-start.1 = ((f32[4,2,2,64,384]{4,3,2,1,0:T(8,128)}), f32[4,2,2,64,384]{4,3,2,1,0:T(8,128)}, u32[]{:S(2)}, u32[]{:S(2)}) async-start(f32[4,2,2,64,384]{4,3,2,1,0:T(8,128)} %broadcast_in_dim.10), calls=%async_computation.1 | async-start | bytes 3145728 | tf_op jit(solution)/shard_map/all_to_all | solution.py:37
  36.1 1.1 pad_maximum_fusion
  37.2 1.9 %collective-permute-start = (f32[2,384,384]{2,1,0:T(8,128)}, f32[2,384,384]{2,1,0:T(8,128)S(1)}, u32[]{:S(2)}, u32[]{:S(2)}) collective-permute-start(f32[2,384,384]{2,1,0:T(8,128)} %pad_maximum_fusion), channel_id=1, source_target_pairs={{0,32},{32,0},{1,33},{33,1},{2,34},{34,2},{3,35},{35,3},{4,36},{36... | collective-permute-start | bytes 3538952 | tf_op jit(solution)/shard_map/ppermute | solution.py:33
  39.1 9.8 %all-to-all-done.1 = f32[4,2,2,64,384]{4,3,2,1,0:T(8,128)} async-done(((f32[4,2,2,64,384]{4,3,2,1,0:T(8,128)}), f32[4,2,2,64,384]{4,3,2,1,0:T(8,128)}, u32[]{:S(2)}, u32[]{:S(2)}) %all-to-all-start.1) | async-done | bytes 1572896 | tf_op jit(solution)/shard_map/all_to_all | solution.py:37
  48.9 1.5 fusion.25
  50.3 0.0 copy-start.8
  50.3 0.0 copy-start.6
  50.4 0.0 collective-permute-done
  50.4 0.6 fusion.13
  50.9 0.5 fusion.18
  51.5 0.6 convolution_add_fusion
  52.1 0.5 convolution_add_fusion.1
  52.6 0.1 maximum_bitcast_fusion.1
  52.7 28.9 %all_to_all.31 = f32[8,2,32,384]{3,2,1,0:T(8,128)} all-to-all(f32[8,2,32,384]{3,2,1,0:T(8,128)S(1)} %maximum_bitcast_fusion.1), channel_id=1, replica_groups=mesh['y'=8,'core'=2,'zh'=4,'zl'=2,'xh'=2,'xl'=2] {'y'}, dimensions={0} | all-to-all | bytes 1572864 | tf_op jit(solution)/shard_map/all_to_all | solution.py:37
  81.6 1.2 reduce_sum.27
  82.8 0.1 broadcast_in_dim.22
  82.9 22.7 %all_to_all.32 = f32[8,2,32,384]{3,2,1,0:T(8,128)S(1)} all-to-all(f32[8,2,32,384]{3,2,1,0:T(8,128)S(1)} %broadcast_in_dim.22), channel_id=1, replica_groups=mesh['y'=8,'core'=2,'zh'=4,'zl'=2,'xh'=2,'xl'=2] {'y'}, dimensions={0} | all-to-all | bytes 1572864 | tf_op jit(solution)/shard_map/all_to_all | solution.py:37
  105.6 0.1 fusion.26
  105.7 0.6 convolution_bitcast_fusion
  106.2 0.6 convolution_bitcast_fusion.2
  106.8 0.5 convolution_bitcast_fusion.1
  107.3 0.5 convolution_bitcast_fusion.3
  107.9 0.1 maximum_bitcast_fusion
  108.0 1.3 copy.17
  109.3 7.9 %all-to-all-start.4 = ((f32[4,2,2,64,384]{4,3,2,1,0:T(8,128)}), f32[4,2,2,64,384]{4,3,2,1,0:T(8,128)S(1)}, u32[]{:S(2)}, u32[]{:S(2)}) async-start(f32[4,2,2,64,384]{4,3,2,1,0:T(8,128)} %copy.17), calls=%async_computation.4 | async-start | bytes 3145728 | tf_op jit(solution)/shard_map/all_to_all | solution.py:37
  117.2 1.6 %fusion.28 = f32[384,384]{1,0:T(8,128)S(1)} fusion(f32[256,384]{1,0:T(8,128)} %bitcast.131, f32[256,384]{1,0:T(8,128)S(1)} %bitcast.122), kind=kOutput, calls=%fused_computation.44 | convolution fusion | flops 226492416 | bytes 1376256 | tf_op jit(solution)/shard_map/dot_general | solution.py:27
  118.8 0.0 copy-start.9
  118.8 0.5 fusion.27
  119.4 0.0 copy-start.2
  119.4 0.5 fusion.30
  119.9 0.5 fusion.29
  120.5 0.0 copy-start.4
  120.5 0.2 select_bitcast_fusion
  120.7 0.6 copy-done.4
  121.3 1.1 pad_maximum_fusion.1
  122.4 1.9 %collective-permute-start.1 = (f32[2,384,384]{2,1,0:T(8,128)}, f32[2,384,384]{2,1,0:T(8,128)}, u32[]{:S(2)}, u32[]{:S(2)}) collective-permute-start(f32[2,384,384]{2,1,0:T(8,128)} %pad_maximum_fusion.1), channel_id=1, source_target_pairs={{0,32},{32,0},{1,33},{33,1},{2,34},{34,2},{3,35},{35,3},{4,36},{36... | collective-permute-start | bytes 3538952 | tf_op jit(solution)/shard_map/ppermute | solution.py:33
  124.3 5.3 %all-to-all-done.4 = f32[4,2,2,64,384]{4,3,2,1,0:T(8,128)S(1)} async-done(((f32[4,2,2,64,384]{4,3,2,1,0:T(8,128)}), f32[4,2,2,64,384]{4,3,2,1,0:T(8,128)S(1)}, u32[]{:S(2)}, u32[]{:S(2)}) %all-to-all-start.4) | async-done | bytes 1572896 | tf_op jit(solution)/shard_map/all_to_all | solution.py:37
  129.5 0.1 reduce_sum.28
  129.7 0.0 copy-start.3
  129.7 0.0 copy-start.5
  129.7 0.8 copy.18
  130.5 4.8 %all-to-all-start.5 = ((f32[16,2,8,384]{3,2,1,0:T(8,128)}), f32[16,2,8,384]{3,2,1,0:T(8,128)S(1)}, u32[]{:S(2)}, u32[]{:S(2)}) async-start(f32[16,2,8,384]{3,2,1,0:T(8,128)} %bitcast.34), calls=%async_computation.5 | async-start | bytes 786432 | tf_op jit(solution)/shard_map/all_to_all | solution.py:37
  135.3 2.4 %fusion = (f32[384,384]{1,0:T(8,128)}, f32[384,384]{1,0:T(8,128)}) fusion(f32[2,384,384]{2,1,0:T(8,128)} %collective-permute-done.1, f32[384,384]{1,0:T(8,128)S(1)} %fusion.30, f32[384,384]{1,0:T(8,128)S(1)} %copy-done.5, pred[]{:T(512)S(6)} %eq.2, f32[384,384]{1,0:T(8,128)S(1)} %copy-done.3, f32[384,384]{1,0:T(8,128)S(1)} %fusion.28), kind=kLoop, calls=%fused_computation.11 | loop fusion | flops 589824 | bytes 4718593 | tf_op jit(solution)/shard_map/add | solution.py:117
  137.7 11.4 %all-to-all-done.5 = f32[16,2,8,384]{3,2,1,0:T(8,128)S(1)} async-done(((f32[16,2,8,384]{3,2,1,0:T(8,128)}), f32[16,2,8,384]{3,2,1,0:T(8,128)S(1)}, u32[]{:S(2)}, u32[]{:S(2)}) %all-to-all-start.5) | async-done | bytes 393248 | tf_op jit(solution)/shard_map/all_to_all | solution.py:37
  149.2 0.6 slice_bitcast_fusion.4
  (21 shorter events, 0.2 us)
Async XLA Ops:
  30.6 5.5 %copy-start = (f32[384,384]{1,0:T(8,128)S(1)}, f32[384,384]{1,0:T(8,128)}, u32[]{:S(2)}) copy-start(f32[384,384]{1,0:T(8,128)} %param.6) | copy-start | bytes 1769476
  30.6 5.5 %copy-start.1 = (f32[384,384]{1,0:T(8,128)S(1)}, f32[384,384]{1,0:T(8,128)}, u32[]{:S(2)}) copy-start(f32[384,384]{1,0:T(8,128)} %param.7) | copy-start | bytes 1769476
  30.6 18.3 %all-to-all-start.1 = ((f32[4,2,2,64,384]{4,3,2,1,0:T(8,128)}), f32[4,2,2,64,384]{4,3,2,1,0:T(8,128)}, u32[]{:S(2)}, u32[]{:S(2)}) async-start(f32[4,2,2,64,384]{4,3,2,1,0:T(8,128)} %broadcast_in_dim.10), calls=%async_computation.1 | async-start | bytes 3145728 | tf_op jit(solution)/shard_map/all_to_all | solution.py:37
  37.2 13.2 %collective-permute-start = (f32[2,384,384]{2,1,0:T(8,128)}, f32[2,384,384]{2,1,0:T(8,128)S(1)}, u32[]{:S(2)}, u32[]{:S(2)}) collective-permute-start(f32[2,384,384]{2,1,0:T(8,128)} %pad_maximum_fusion), channel_id=1, source_target_pairs={{0,32},{32,0},{1,33},{33,1},{2,34},{34,2},{3,35},{35,3},{4,36},{36... | collective-permute-start | bytes 3538952 | tf_op jit(solution)/shard_map/ppermute | solution.py:33
  50.3 1.1 copy-start.8
  50.3 1.1 copy-start.6
  50.4 2.2 %copy-start.10 = (f32[4,1,1,64,384]{4,3,2,1,0:T(8,128)}, f32[4,1,1,64,384]{4,3,2,1,0:T(8,128)S(1)}, u32[]{:S(2)}) copy-start(f32[4,1,1,64,384]{4,3,2,1,0:T(8,128)S(1)} %get-tuple-element.13) | copy-start | bytes 1179652
  109.3 20.2 %all-to-all-start.4 = ((f32[4,2,2,64,384]{4,3,2,1,0:T(8,128)}), f32[4,2,2,64,384]{4,3,2,1,0:T(8,128)S(1)}, u32[]{:S(2)}, u32[]{:S(2)}) async-start(f32[4,2,2,64,384]{4,3,2,1,0:T(8,128)} %copy.17), calls=%async_computation.4 | async-start | bytes 3145728 | tf_op jit(solution)/shard_map/all_to_all | solution.py:37
  117.2 2.1 %copy-start.7 = (f32[4,1,1,64,384]{4,3,2,1,0:T(8,128)S(1)}, f32[4,1,1,64,384]{4,3,2,1,0:T(8,128)}, u32[]{:S(2)}) copy-start(f32[4,1,1,64,384]{4,3,2,1,0:T(8,128)} %copy-done.6) | copy-start | bytes 1179652
  118.8 1.1 copy-start.9
  119.4 1.1 copy-start.2
  120.5 0.8 copy-start.4
  122.4 12.9 %collective-permute-start.1 = (f32[2,384,384]{2,1,0:T(8,128)}, f32[2,384,384]{2,1,0:T(8,128)}, u32[]{:S(2)}, u32[]{:S(2)}) collective-permute-start(f32[2,384,384]{2,1,0:T(8,128)} %pad_maximum_fusion.1), channel_id=1, source_target_pairs={{0,32},{32,0},{1,33},{33,1},{2,34},{34,2},{3,35},{35,3},{4,36},{36... | collective-permute-start | bytes 3538952 | tf_op jit(solution)/shard_map/ppermute | solution.py:33
  129.7 5.7 %copy-start.3 = (f32[384,384]{1,0:T(8,128)S(1)}, f32[384,384]{1,0:T(8,128)}, u32[]{:S(2)}) copy-start(f32[384,384]{1,0:T(8,128)} %copy-done.2) | copy-start | bytes 1769476
  129.7 5.7 %copy-start.5 = (f32[384,384]{1,0:T(8,128)S(1)}, f32[384,384]{1,0:T(8,128)}, u32[]{:S(2)}) copy-start(f32[384,384]{1,0:T(8,128)} %copy-done.4) | copy-start | bytes 1769476
  130.5 18.7 %all-to-all-start.5 = ((f32[16,2,8,384]{3,2,1,0:T(8,128)}), f32[16,2,8,384]{3,2,1,0:T(8,128)S(1)}, u32[]{:S(2)}, u32[]{:S(2)}) async-start(f32[16,2,8,384]{3,2,1,0:T(8,128)} %bitcast.34), calls=%async_computation.5 | async-start | bytes 786432 | tf_op jit(solution)/shard_map/all_to_all | solution.py:37

commit v3 on v2

v3 whole, which is shorter than its diff:
```python
import math

import jax
import jax.numpy as jnp
from jax import lax
from jax.sharding import Mesh, PartitionSpec as P

precise = lax.Precision.HIGH
Y, CORE, ZH, ZL, XH, XL = 8, 2, 4, 2, 2, 2
N_FAR, N_NEAR, QUAD = ZH * XH, ZL * XL, Y // 2
Z, X = ZH * ZL, XH * XL
CELL = ("core", "zh", "zl", "xh", "xl")
ALL = ("y",) + CELL


def pair_of(c, k, parity):
    return 2 * k + (parity + c) % 2 + c


BLOCKS = [
    [
        (c * Z + pair_of(c, k, (p + c) % 2) % Z) * X + pair_of(c, j, q) % X
        for p in range(2)
        for q in range(2)
    ]
    for c in range(CORE)
    for k in range(ZH)
    for j in range(XH)
]
FAR = [
    [
        (((pair_of(c, k, p) % Y) * CORE + c) * Z + 2 * zh + zl) * X + 2 * xh + xl
        for zh in range(ZH)
        for xh in range(XH)
        for p in range(2)
    ]
    for c in range(CORE)
    for k in range(QUAD)
    for zl in range(ZL)
    for xl in range(XL)
]
PARTNERS = [
    ((pair_of(c, k, p) % Y) * CORE + c, (pair_of(c, k, 1 - p) % Y) * CORE + c)
    for c in range(CORE)
    for k in range(QUAD)
    for p in range(2)
]
QUADS = [list(range(p, Y, 2)) for p in range(2)]


def product(left, right, dims):
    return lax.dot_general(
        left, right, (dims, ((), ())), precision=precise, preferred_element_type=jnp.float32
    )


def swap_cores(block):
    return lax.ppermute(block, "core", [(0, 1), (1, 0)])


def swap_pair(block):
    return lax.ppermute(block, ("y", "core"), PARTNERS)


def exchange(blocks, axis, groups):
    return lax.all_to_all(
        blocks, axis, split_axis=0, concat_axis=0, tiled=True, axis_index_groups=groups
    )


def copies(block, count):
    return jnp.broadcast_to(block[None], (count, *block.shape))


def shards(patches, cotangent, expand_weight, reduce_weight):
    odd = lax.axis_index("y") % 2
    tokens, width = patches.shape
    hidden = expand_weight.shape[1]
    part = tokens // 2
    rows = N_FAR * part

    def own_first(block):
        return jnp.where(odd == 0, block, block[::-1])

    mine = jnp.stack([patches.reshape(2, part, width), cotangent.reshape(2, part, width)], axis=1)
    far = exchange(copies(mine, N_FAR).reshape(2 * N_FAR, 2, part, width), ALL, FAR)
    far = far.reshape(N_FAR, 2, 2, part, width).transpose(1, 2, 0, 3, 4)
    far = own_first(far).reshape(2, 2, rows, width)
    far, other_expand = lax.optimization_barrier((far, swap_pair(expand_weight)))
    inputs = exchange(copies(far, N_NEAR), CELL, BLOCKS)

    expand = (expand_weight, other_expand)
    reduce = (reduce_weight, swap_pair(reduce_weight))

    half = N_NEAR // 2 * rows

    def terms(block):
        def take(pair, array):
            return block[:, pair, array].reshape(half, width)

        return jnp.stack(
            [
                product(take(0, 0), expand[0], ((1,), (0,)))
                + product(take(1, 0), expand[1], ((1,), (0,))),
                product(take(0, 1), reduce[0], ((1,), (1,)))
                + product(take(1, 1), reduce[1], ((1,), (1,))),
            ]
        )

    away = swap_cores(terms(inputs[N_NEAR // 2 :]))
    share = half // QUAD
    summed = (terms(inputs[: N_NEAR // 2]) + away).reshape(2, QUAD, share, hidden)
    preact, act_grad = jnp.sum(exchange(summed.transpose(1, 0, 2, 3), "y", QUADS), axis=0)
    act_cdf = 0.5 * (1.0 + jax.scipy.special.erf(preact / math.sqrt(2.0)))
    activated = preact * act_cdf
    pre_grad = act_grad * (
        act_cdf + preact * jnp.exp(-0.5 * preact * preact) / math.sqrt(2.0 * math.pi)
    )
    own = exchange(copies(jnp.stack([activated, pre_grad]), QUAD), "y", QUADS)
    other = swap_cores(own)

    def results(both):
        active, pregrad = (both[:, k].reshape(half, hidden) for k in range(2))
        return jnp.stack(
            [
                jnp.stack(
                    [
                        product(active, reduce[p], ((1,), (0,))),
                        product(pregrad, expand[p], ((1,), (1,))),
                    ]
                ).reshape(2, N_NEAR // 2, rows, width)
                for p in range(2)
            ]
        )

    outs = jnp.concatenate([results(own), results(other)], axis=2)
    outs = outs.transpose(2, 0, 1, 3, 4)
    outs, own, other = lax.optimization_barrier((outs, own, other))
    near = jnp.sum(exchange(outs, CELL, BLOCKS), axis=0)
    near = own_first(near).reshape(2, 2, N_FAR, part, width).transpose(2, 0, 1, 3, 4)

    flat = [
        jnp.concatenate([own[:, k].reshape(half, hidden), other[:, k].reshape(half, hidden)])
        for k in range(2)
    ]
    grads = [
        jnp.stack(
            [
                product(inputs[:, p, 0].reshape(2 * half, width), flat[1], ((0,), (0,))),
                product(flat[0], inputs[:, p, 1].reshape(2 * half, width), ((0,), (0,))),
            ]
        )
        for p in range(2)
    ]
    away = swap_pair(grads[1])
    last = exchange(near.reshape(2 * N_FAR, 2, part, width), ALL, FAR)
    last = jnp.sum(last.reshape(N_FAR, 2, 2, part, width), axis=0)
    mlp_output, patch_grad = (last[:, k].reshape(tokens, width) for k in range(2))
    return mlp_output, patch_grad, grads[0][0] + away[0], grads[0][1] + away[1]


def solution(mesh):
    fine = Mesh(mesh.devices.reshape(Y, CORE, ZH, ZL, XH, XL), ALL)
    row, col = ("y", "core"), ("zh", "zl", "xh", "xl")
    placed = (P(col, row), P(col, row), P(row, col), P(col, row))
    return jax.shard_map(
        shards, mesh=fine, in_specs=placed, out_specs=placed, check_vma=False
    )
```

time: 152 us -> 144 us (0.947); the launches traced: 150 us -> 143 us
  blocking collectives: 79.4 us -> 30.5 us
  starting transfers between devices: 22.1 us -> 52.9 us
  matrix products: 7.46 us -> 16.3 us
  waiting for transfers between devices: 26.4 us -> 33 us
  other arithmetic: 7.11 us -> 3.32 us
    all_to_all x3 -> x2, blocking collectives: 79.4 us -> 30.5 us  [exchange(): lax.all_to_all(blocks, axis, split_axis=0, concat_axis=0, tiled=True, axi...]
    ppermute x0 -> x3, starting transfers between devices: none -> 12.8 us  [swap_pair(): return lax.ppermute(block, ('y', 'core'), PARTNERS)]
    all_to_all x3 -> x4, starting transfers between devices: 18.2 us -> 30.9 us  [exchange(): lax.all_to_all(blocks, axis, split_axis=0, concat_axis=0, tiled=True, axi...]
    dot_general x12 -> x20, matrix products: 7.46 us -> 16.3 us  [product(): lax.dot_general(left, right, (dims, ((), ())), precision=precise, preferr...]
    ppermute x2, starting transfers between devices: 3.82 us -> 9.16 us  [swap_cores(): return lax.ppermute(block, 'core', [(0, 1), (1, 0)])]
    ppermute x0 -> x3, waiting for transfers between devices: none -> 4.23 us  [swap_pair(): return lax.ppermute(block, ('y', 'core'), PARTNERS)]
    add x1, other arithmetic: 2.41 us -> 0.04 us  [shards(): terms(inputs[:N_NEAR // 2]) + away]
    all_to_all x3 -> x4, waiting for transfers between devices: 26.4 us -> 28.8 us  [exchange(): lax.all_to_all(blocks, axis, split_axis=0, concat_axis=0, tiled=True, axi...]
  transfers between devices with their start and end apart: 5 -> 9, of which waited for: 3 -> 5; matrix products, arithmetic and copies ran while one was open for 7% -> 10% of each run, Pallas kernels for 0% -> 0%
where the time goes in v3:
time: 144 us; the launch traced here: 143 us
  starting transfers between devices  52.9 us (37%)
  waiting for transfers between devices  33 us (23%)
  blocking collectives  30.5 us (21%)
  matrix products  16.3 us (11%)
  local copies, waits for them, and re-layouts  6.38 us (4%)
  other arithmetic  3.32 us (2%)
    all_to_all x4, starting transfers between devices, exchange(): lax.all_to_all(blocks, axis, split_axis=0, concat_axis=0, tiled=True, axi...  30.9 us
    all_to_all x2, blocking collectives, exchange(): lax.all_to_all(blocks, axis, split_axis=0, concat_axis=0, tiled=True, axi...  30.5 us
    all_to_all x4, waiting for transfers between devices, exchange(): lax.all_to_all(blocks, axis, split_axis=0, concat_axis=0, tiled=True, axi...  28.8 us
    dot_general x20, matrix products, product(): lax.dot_general(left, right, (dims, ((), ())), precision=precise, preferr...  16.3 us
    ppermute x3, starting transfers between devices, swap_pair(): return lax.ppermute(block, ('y', 'core'), PARTNERS)  12.8 us
    ppermute x2, starting transfers between devices, swap_cores(): return lax.ppermute(block, 'core', [(0, 1), (1, 0)])  9.16 us
    ppermute x3, waiting for transfers between devices, swap_pair(): return lax.ppermute(block, ('y', 'core'), PARTNERS)  4.23 us
  transfers between devices with their start and end apart: 9, of which 5 were waited for; matrix products, arithmetic and copies ran while one was open for 10% of the time, Pallas kernels for 0%

profile of v3, /device:TPU:1, one launch (start us, length us, event | category | flops | bytes accessed | tf_op | source)
XLA Modules:
  0.0 143.3 jit_solution(936918456181935936)
XLA Ops:
  0.6 0.8 pad_maximum_fusion.13
  1.4 0.8 broadcast_in_dim.6
  2.2 16.3 %all-to-all-start = ((f32[16,2,8,384]{3,2,1,0:T(8,128)}), f32[16,2,8,384]{3,2,1,0:T(8,128)S(1)}, u32[]{:S(2)}, u32[]{:S(2)}) async-start(f32[16,2,8,384]{3,2,1,0:T(8,128)} %bitcast.2), calls=%async_computation | async-start | bytes 786432 | tf_op jit(solution)/shard_map/all_to_all | solution.py:66
  18.5 4.5 %collective-permute-start = (f32[384,384]{1,0:T(8,128)}, f32[384,384]{1,0:T(8,128)S(1)}, u32[]{:S(2)}, u32[]{:S(2)}) collective-permute-start(f32[384,384]{1,0:T(8,128)} %param.6), channel_id=1, source_target_pairs={{0,64},{64,0},{128,192},{192,128},{256,320},{320,256},{384,448},{4... | collective-permute-start | bytes 1769480 | tf_op jit(solution)/shard_map/ppermute | solution.py:62
  23.0 10.6 %all-to-all-done = f32[16,2,8,384]{3,2,1,0:T(8,128)S(1)} async-done(((f32[16,2,8,384]{3,2,1,0:T(8,128)}), f32[16,2,8,384]{3,2,1,0:T(8,128)S(1)}, u32[]{:S(2)}, u32[]{:S(2)}) %all-to-all-start) | async-done | bytes 393248 | tf_op jit(solution)/shard_map/all_to_all | solution.py:66
  33.6 1.3 broadcast_in_dim.7
  35.0 5.5 %all-to-all-start.1 = ((f32[4,2,2,64,384]{4,3,2,1,0:T(8,128)}), f32[4,2,2,64,384]{4,3,2,1,0:T(8,128)S(1)}, u32[]{:S(2)}, u32[]{:S(2)}) async-start(f32[4,2,2,64,384]{4,3,2,1,0:T(8,128)} %broadcast_in_dim.7), calls=%async_computation.1 | async-start | bytes 3145728 | tf_op jit(solution)/shard_map/all_to_all | solution.py:66
  40.5 5.7 %collective-permute-start.1 = (f32[384,384]{1,0:T(8,128)S(1)}, f32[384,384]{1,0:T(8,128)}, u32[]{:S(2)}, u32[]{:S(2)}) collective-permute-start(f32[384,384]{1,0:T(8,128)S(1)} %copy-done.1), channel_id=1, source_target_pairs={{0,64},{64,0},{128,192},{192,128},{256,320},{320,256},{384,448},{4... | collective-permute-start | bytes 1769480 | tf_op jit(solution)/shard_map/ppermute | solution.py:62
  46.2 6.2 %all-to-all-done.1 = f32[4,2,2,64,384]{4,3,2,1,0:T(8,128)S(1)} async-done(((f32[4,2,2,64,384]{4,3,2,1,0:T(8,128)}), f32[4,2,2,64,384]{4,3,2,1,0:T(8,128)S(1)}, u32[]{:S(2)}, u32[]{:S(2)}) %all-to-all-start.1) | async-done | bytes 1572896 | tf_op jit(solution)/shard_map/all_to_all | solution.py:66
  52.4 0.1 fusion.27
  52.6 0.4 fusion.34
  53.0 0.4 fusion.1
  53.3 0.4 fusion.32
  53.7 0.4 fusion.35
  54.1 1.5 %fusion = f32[1,128,384]{2,1,0:T(8,128)S(1)} fusion(f32[128,384]{1,0:T(8,128)S(1)} %fusion.35, f32[128,384]{1,0:T(8,128)S(1)} %bitcast.154, f32[384,384]{1,0:T(8,128)} %collective-permute-done.1), kind=kOutput, calls=%fused_computation.13 | convolution fusion | flops 113295360 | bytes 1179648 | tf_op jit(solution)/shard_map/dot_general | solution.py:52
  55.6 1.9 %collective-permute-start.2 = (f32[2,128,384]{2,1,0:T(8,128)S(1)}, f32[2,128,384]{2,1,0:T(8,128)S(1)}, u32[]{:S(2)}, u32[]{:S(2)}) collective-permute-start(f32[2,128,384]{2,1,0:T(8,128)S(1)} %pad_maximum_fusion.1), channel_id=1, source_target_pairs={{0,32},{32,0},{1,33},{33,1},{2,34},{34,2},{3,35},{35,3},{4,36},{36... | collective-permute-start | bytes 1179656 | tf_op jit(solution)/shard_map/ppermute | solution.py:58
  57.6 0.4 fusion.3
  57.9 0.4 fusion.33
  58.4 1.5 %fusion.2 = f32[1,128,384]{2,1,0:T(8,128)S(1)} fusion(f32[128,384]{1,0:T(8,128)S(1)} %fusion.33, f32[128,384]{1,0:T(8,128)S(1)} %bitcast.152, f32[384,384]{1,0:T(8,128)} %collective-permute-done.1), kind=kOutput, calls=%fused_computation.17 | convolution fusion | flops 113295360 | bytes 1179648 | tf_op jit(solution)/shard_map/dot_general | solution.py:52
  59.9 16.2 %all_to_all.30 = f32[4,2,32,384]{3,2,1,0:T(8,128)} all-to-all(f32[4,2,32,384]{3,2,1,0:T(8,128)S(1)} %bitcast.147), channel_id=1, replica_groups={{0,128,256,384},{64,192,320,448},{1,129,257,385},{65,193,321,449},{2,13..., dimensions={0} | all-to-all | bytes 786432 | tf_op jit(solution)/shard_map/all_to_all | solution.py:66
  76.1 1.0 reduce_sum.27
  77.2 14.3 %all_to_all.31 = f32[4,2,32,384]{3,2,1,0:T(8,128)S(1)} all-to-all(f32[4,2,32,384]{3,2,1,0:T(8,128)S(1)} %broadcast_in_dim.8), channel_id=1, replica_groups={{0,128,256,384},{64,192,320,448},{1,129,257,385},{65,193,321,449},{2,13..., dimensions={0} | all-to-all | bytes 786432 | tf_op jit(solution)/shard_map/all_to_all | solution.py:66
  91.6 0.4 convolution_bitcast_fusion.6
  92.0 7.2 %collective-permute-start.3 = (f32[4,2,32,384]{3,2,1,0:T(8,128)S(1)}, f32[4,2,32,384]{3,2,1,0:T(8,128)S(1)}, u32[]{:S(2)}, u32[]{:S(2)}) collective-permute-start(f32[4,2,32,384]{3,2,1,0:T(8,128)S(1)} %all_to_all.31), channel_id=1, source_target_pairs={{0,32},{32,0},{1,33},{33,1},{2,34},{34,2},{3,35},{35,3},{4,36},{36... | collective-permute-start | bytes 1179656 | tf_op jit(solution)/shard_map/ppermute | solution.py:58
  99.2 0.4 convolution_bitcast_fusion.8
  99.6 0.4 convolution_bitcast_fusion.9
  100.0 1.4 convolution_bitcast_fusion.7
  101.5 0.4 convolution_bitcast_fusion.2
  101.9 0.4 convolution_bitcast_fusion.4
  102.3 0.4 convolution_bitcast_fusion.5
  102.7 1.4 convolution_bitcast_fusion.3
  104.2 0.1 maximum_bitcast_fusion
  104.3 1.3 copy.16
  105.6 4.3 %all-to-all-start.4 = ((f32[4,2,2,64,384]{4,3,2,1,0:T(8,128)}), f32[4,2,2,64,384]{4,3,2,1,0:T(8,128)S(1)}, u32[]{:S(2)}, u32[]{:S(2)}) async-start(f32[4,2,2,64,384]{4,3,2,1,0:T(8,128)} %copy.16), calls=%async_computation.4 | async-start | bytes 3145728 | tf_op jit(solution)/shard_map/all_to_all | solution.py:66
  109.9 0.9 fusion.26
  110.9 0.3 copy-done.5
  111.2 0.5 convolution_bitcast_fusion.1
  111.8 0.5 convolution_bitcast_fusion
  112.3 1.1 pad_maximum_fusion
  113.4 2.6 %collective-permute-start.4 = (f32[2,384,384]{2,1,0:T(8,128)}, f32[2,384,384]{2,1,0:T(8,128)}, u32[]{:S(2)}, u32[]{:S(2)}) collective-permute-start(f32[2,384,384]{2,1,0:T(8,128)} %pad_maximum_fusion), channel_id=1, source_target_pairs={{0,64},{64,0},{128,192},{192,128},{256,320},{320,256},{384,448},{4... | collective-permute-start | bytes 3538952 | tf_op jit(solution)/shard_map/ppermute | solution.py:62
  116.0 5.9 %all-to-all-done.4 = f32[4,2,2,64,384]{4,3,2,1,0:T(8,128)S(1)} async-done(((f32[4,2,2,64,384]{4,3,2,1,0:T(8,128)}), f32[4,2,2,64,384]{4,3,2,1,0:T(8,128)S(1)}, u32[]{:S(2)}, u32[]{:S(2)}) %all-to-all-start.4) | async-done | bytes 1572896 | tf_op jit(solution)/shard_map/all_to_all | solution.py:66
  122.1 0.8 copy.17
  122.8 4.8 %all-to-all-start.5 = ((f32[16,2,8,384]{3,2,1,0:T(8,128)}), f32[16,2,8,384]{3,2,1,0:T(8,128)S(1)}, u32[]{:S(2)}, u32[]{:S(2)}) async-start(f32[16,2,8,384]{3,2,1,0:T(8,128)} %bitcast.40), calls=%async_computation.5 | async-start | bytes 786432 | tf_op jit(solution)/shard_map/all_to_all | solution.py:66
  127.7 4.2 %collective-permute-done.4 = f32[2,384,384]{2,1,0:T(8,128)} collective-permute-done((f32[2,384,384]{2,1,0:T(8,128)}, f32[2,384,384]{2,1,0:T(8,128)}, u32[]{:S(2)}, u32[]{:S(2)}) %collective-permute-start.4) | collective-permute-done | bytes 1179680 | tf_op jit(solution)/shard_map/ppermute | solution.py:62
  131.9 2.4 %fusion.4 = f32[384,384]{1,0:T(8,128)} fusion(f32[2,384,384]{2,1,0:T(8,128)} %collective-permute-done.4, f32[256,384]{1,0:T(8,128)S(1)} %bitcast.151, f32[128,384]{1,0:T(8,128)S(1)} %bitcast.143, f32[128,384]{1,0:T(8,128)S(1)} %bitcast.141), kind=kOutput, calls=%fused_computation.23 | convolution fusion | flops 226738176 | bytes 1966080 | tf_op jit(solution)/shard_map/dot_general | solution.py:52
  134.3 2.4 %fusion.5 = f32[384,384]{1,0:T(8,128)} fusion(f32[2,384,384]{2,1,0:T(8,128)} %collective-permute-done.4, f32[256,384]{1,0:T(8,128)S(1)} %bitcast.150, f32[128,384]{1,0:T(8,128)S(1)} %bitcast.139, f32[128,384]{1,0:T(8,128)S(1)} %bitcast.137), kind=kOutput, calls=%fused_computation.25 | convolution fusion | flops 226738176 | bytes 1966080 | tf_op jit(solution)/shard_map/dot_general | solution.py:52
  136.7 6.0 %all-to-all-done.5 = f32[16,2,8,384]{3,2,1,0:T(8,128)S(1)} async-done(((f32[16,2,8,384]{3,2,1,0:T(8,128)}), f32[16,2,8,384]{3,2,1,0:T(8,128)S(1)}, u32[]{:S(2)}, u32[]{:S(2)}) %all-to-all-start.5) | async-done | bytes 393248 | tf_op jit(solution)/shard_map/all_to_all | solution.py:66
  142.7 0.6 slice_bitcast_fusion.2
  (31 shorter events, 0.6 us)
Async XLA Ops:
  2.2 31.4 %all-to-all-start = ((f32[16,2,8,384]{3,2,1,0:T(8,128)}), f32[16,2,8,384]{3,2,1,0:T(8,128)S(1)}, u32[]{:S(2)}, u32[]{:S(2)}) async-start(f32[16,2,8,384]{3,2,1,0:T(8,128)} %bitcast.2), calls=%async_computation | async-start | bytes 786432 | tf_op jit(solution)/shard_map/all_to_all | solution.py:66
  18.5 15.1 %collective-permute-start = (f32[384,384]{1,0:T(8,128)}, f32[384,384]{1,0:T(8,128)S(1)}, u32[]{:S(2)}, u32[]{:S(2)}) collective-permute-start(f32[384,384]{1,0:T(8,128)} %param.6), channel_id=1, source_target_pairs={{0,64},{64,0},{128,192},{192,128},{256,320},{320,256},{384,448},{4... | collective-permute-start | bytes 1769480 | tf_op jit(solution)/shard_map/ppermute | solution.py:62
  35.0 5.5 %copy-start.1 = (f32[384,384]{1,0:T(8,128)S(1)}, f32[384,384]{1,0:T(8,128)}, u32[]{:S(2)}) copy-start(f32[384,384]{1,0:T(8,128)} %param.7) | copy-start | bytes 1769476
  35.0 17.5 %all-to-all-start.1 = ((f32[4,2,2,64,384]{4,3,2,1,0:T(8,128)}), f32[4,2,2,64,384]{4,3,2,1,0:T(8,128)S(1)}, u32[]{:S(2)}, u32[]{:S(2)}) async-start(f32[4,2,2,64,384]{4,3,2,1,0:T(8,128)} %broadcast_in_dim.7), calls=%async_computation.1 | async-start | bytes 3145728 | tf_op jit(solution)/shard_map/all_to_all | solution.py:66
  40.5 12.1 %copy-start = (f32[384,384]{1,0:T(8,128)S(1)}, f32[384,384]{1,0:T(8,128)}, u32[]{:S(2)}) copy-start(f32[384,384]{1,0:T(8,128)} %param.6) | copy-start | bytes 1769476
  40.5 13.6 %collective-permute-start.1 = (f32[384,384]{1,0:T(8,128)S(1)}, f32[384,384]{1,0:T(8,128)}, u32[]{:S(2)}, u32[]{:S(2)}) collective-permute-start(f32[384,384]{1,0:T(8,128)S(1)} %copy-done.1), channel_id=1, source_target_pairs={{0,64},{64,0},{128,192},{192,128},{256,320},{320,256},{384,448},{4... | collective-permute-start | bytes 1769480 | tf_op jit(solution)/shard_map/ppermute | solution.py:62
  55.6 4.2 %collective-permute-start.2 = (f32[2,128,384]{2,1,0:T(8,128)S(1)}, f32[2,128,384]{2,1,0:T(8,128)S(1)}, u32[]{:S(2)}, u32[]{:S(2)}) collective-permute-start(f32[2,128,384]{2,1,0:T(8,128)S(1)} %pad_maximum_fusion.1), channel_id=1, source_target_pairs={{0,32},{32,0},{1,33},{33,1},{2,34},{34,2},{3,35},{35,3},{4,36},{36... | collective-permute-start | bytes 1179656 | tf_op jit(solution)/shard_map/ppermute | solution.py:58
  91.5 8.5 %copy-start.2 = (f32[4,2,32,384]{3,2,1,0:T(8,128)}, f32[4,2,32,384]{3,2,1,0:T(8,128)S(1)}, u32[]{:S(2)}) copy-start(f32[4,2,32,384]{3,2,1,0:T(8,128)S(1)} %all_to_all.31) | copy-start | bytes 1179652
  92.0 9.5 %collective-permute-start.3 = (f32[4,2,32,384]{3,2,1,0:T(8,128)S(1)}, f32[4,2,32,384]{3,2,1,0:T(8,128)S(1)}, u32[]{:S(2)}, u32[]{:S(2)}) collective-permute-start(f32[4,2,32,384]{3,2,1,0:T(8,128)S(1)} %all_to_all.31), channel_id=1, source_target_pairs={{0,32},{32,0},{1,33},{33,1},{2,34},{34,2},{3,35},{35,3},{4,36},{36... | collective-permute-start | bytes 1179656 | tf_op jit(solution)/shard_map/ppermute | solution.py:58
  101.5 1.2 copy-start.4
  105.6 16.3 %all-to-all-start.4 = ((f32[4,2,2,64,384]{4,3,2,1,0:T(8,128)}), f32[4,2,2,64,384]{4,3,2,1,0:T(8,128)S(1)}, u32[]{:S(2)}, u32[]{:S(2)}) async-start(f32[4,2,2,64,384]{4,3,2,1,0:T(8,128)} %copy.16), calls=%async_computation.4 | async-start | bytes 3145728 | tf_op jit(solution)/shard_map/all_to_all | solution.py:66
  109.9 1.0 copy-start.3
  109.9 1.3 copy-start.5
  113.4 18.5 %collective-permute-start.4 = (f32[2,384,384]{2,1,0:T(8,128)}, f32[2,384,384]{2,1,0:T(8,128)}, u32[]{:S(2)}, u32[]{:S(2)}) collective-permute-start(f32[2,384,384]{2,1,0:T(8,128)} %pad_maximum_fusion), channel_id=1, source_target_pairs={{0,64},{64,0},{128,192},{192,128},{256,320},{320,256},{384,448},{4... | collective-permute-start | bytes 3538952 | tf_op jit(solution)/shard_map/ppermute | solution.py:62
  122.0 9.9 %copy-start.6 = (f32[4,1,1,64,384]{4,3,2,1,0:T(8,128)S(1)}, f32[4,1,1,64,384]{4,3,2,1,0:T(8,128)}, u32[]{:S(2)}) copy-start(f32[4,1,1,64,384]{4,3,2,1,0:T(8,128)} %get-tuple-element.14) | copy-start | bytes 1179652
  122.8 19.8 %all-to-all-start.5 = ((f32[16,2,8,384]{3,2,1,0:T(8,128)}), f32[16,2,8,384]{3,2,1,0:T(8,128)S(1)}, u32[]{:S(2)}, u32[]{:S(2)}) async-start(f32[16,2,8,384]{3,2,1,0:T(8,128)} %bitcast.40), calls=%async_computation.5 | async-start | bytes 786432 | tf_op jit(solution)/shard_map/all_to_all | solution.py:66

commit v4 on v3

--- a/solution.py
+++ b/solution.py
@@ -1,8 +1,11 @@
+import functools
 import math
 
 import jax
 import jax.numpy as jnp
 from jax import lax
+from jax.experimental import pallas as pl
+from jax.experimental.pallas import tpu as pltpu
 from jax.sharding import Mesh, PartitionSpec as P
 
 precise = lax.Precision.HIGH
@@ -54,6 +57,98 @@
     )
 
 
+def halves(block):
+    high = block.astype(jnp.bfloat16)
+    return high, (block - high.astype(jnp.float32)).astype(jnp.bfloat16)
+
+
+def product_of_halves(left, right, flipped):
+    dims = (((1,), (1 if flipped else 0,)), ((), ()))
+
+    def dot(a, b):
+        return lax.dot_general(a, b, dims, preferred_element_type=jnp.float32)
+
+    return dot(left[0], right[0]) + (dot(left[0], right[1]) + dot(left[1], right[0]))
+
+
+def terms_kernel(first, share, inputs, expand, expand_far, reduce, reduce_far, out):
+    weights = ((expand, expand_far), (reduce, reduce_far))
+    for array in range(2):
+        total = None
+        for pair in range(2):
+            block = jnp.concatenate([inputs[first + n, pair, array] for n in range(2)], axis=0)
+            term = product_of_halves(
+                halves(block), halves(weights[array][pair][...]), array == 1
+            )
+            total = term if total is None else total + term
+        for q in range(QUAD):
+            out[q, array] = total[q * share : (q + 1) * share]
+
+
+def results_kernel(earlier, both, expand, expand_far, reduce, reduce_far, out):
+    at = 0
+    if earlier is not None:
+        at = earlier.shape[0]
+        out[:at] = earlier[...]
+    rows = out.shape[3]
+    weights = ((reduce, reduce_far), (expand, expand_far))
+    for array in range(2):
+        block = halves(jnp.concatenate([both[q, array] for q in range(QUAD)], axis=0))
+        for pair in range(2):
+            term = product_of_halves(block, halves(weights[array][pair][...]), array == 1)
+            for n in range(2):
+                out[at + n, pair, array] = term[n * rows : (n + 1) * rows]
+
+
+def send_kernel(patches, cotangent, out):
+    part = out.shape[3]
+    for p in range(2):
+        for array, source in enumerate((patches, cotangent)):
+            block = source[p * part : (p + 1) * part]
+            for m in range(N_FAR):
+                out[m, p, array] = block
+
+
+def spread_kernel(odd, far, out):
+    part = far.shape[3]
+    for p in range(2):
+        source = jnp.bitwise_xor(odd[0], p)
+        for array in range(2):
+            for m in range(N_FAR):
+                block = far[m, source, array]
+                for n in range(N_NEAR):
+                    out[n, p, array, m * part : (m + 1) * part] = block
+
+
+def fold_kernel(odd, near, out):
+    part = out.shape[3]
+    for p in range(2):
+        target = jnp.bitwise_xor(odd[0], p)
+        for array in range(2):
+            total = (near[0, p, array] + near[1, p, array]) + (
+                near[2, p, array] + near[3, p, array]
+            )
+            for m in range(N_FAR):
+                out[m, target, array] = total[m * part : (m + 1) * part]
+
+
+def local_call(kernel, shape, flops, *operands):
+    bytes_accessed = 4 * (math.prod(shape) + sum(v.size for v in operands))
+    return pl.pallas_call(
+        kernel,
+        out_shape=jax.ShapeDtypeStruct(shape, jnp.float32),
+        in_specs=[
+            pl.BlockSpec(memory_space=pltpu.SMEM if v.dtype == jnp.int32 else pltpu.VMEM)
+            for v in operands
+        ],
+        out_specs=pl.BlockSpec(memory_space=pltpu.VMEM),
+        compiler_params=pltpu.CompilerParams(vmem_limit_bytes=8 * 2**20),
+        cost_estimate=pl.CostEstimate(
+            flops=flops, bytes_accessed=bytes_accessed, transcendentals=0
+        ),
+    )(*operands)
+
+
 def swap_cores(block):
     return lax.ppermute(block, "core", [(0, 1), (1, 0)])
 
@@ -73,44 +168,39 @@
 
 
 def shards(patches, cotangent, expand_weight, reduce_weight):
-    odd = lax.axis_index("y") % 2
+    odd = (lax.axis_index("y") % 2).reshape(1)
     tokens, width = patches.shape
     hidden = expand_weight.shape[1]
     part = tokens // 2
     rows = N_FAR * part
 
-    def own_first(block):
-        return jnp.where(odd == 0, block, block[::-1])
-
-    mine = jnp.stack([patches.reshape(2, part, width), cotangent.reshape(2, part, width)], axis=1)
-    far = exchange(copies(mine, N_FAR).reshape(2 * N_FAR, 2, part, width), ALL, FAR)
-    far = far.reshape(N_FAR, 2, 2, part, width).transpose(1, 2, 0, 3, 4)
-    far = own_first(far).reshape(2, 2, rows, width)
+    mine = local_call(send_kernel, (N_FAR, 2, 2, part, width), 0, patches, cotangent)
+    far = exchange(mine.reshape(2 * N_FAR, 2, part, width), ALL, FAR)
+    far = far.reshape(N_FAR, 2, 2, part, width)
     far, other_expand = lax.optimization_barrier((far, swap_pair(expand_weight)))
-    inputs = exchange(copies(far, N_NEAR), CELL, BLOCKS)
+    inputs = local_call(spread_kernel, (N_NEAR, 2, 2, rows, width), 0, odd, far)
+    inputs = exchange(inputs, CELL, BLOCKS)
 
     expand = (expand_weight, other_expand)
     reduce = (reduce_weight, swap_pair(reduce_weight))
 
     half = N_NEAR // 2 * rows
-
-    def terms(block):
-        def take(pair, array):
-            return block[:, pair, array].reshape(half, width)
-
-        return jnp.stack(
-            [
-                product(take(0, 0), expand[0], ((1,), (0,)))
-                + product(take(1, 0), expand[1], ((1,), (0,))),
-                product(take(0, 1), reduce[0], ((1,), (1,)))
-                + product(take(1, 1), reduce[1], ((1,), (1,))),
-            ]
+    share = half // QUAD
+    flops = 3 * 2 * 4 * half * width * hidden
+    weights = (*expand, *reduce)
+
+    def terms(first):
+        return local_call(
+            functools.partial(terms_kernel, first, share),
+            (QUAD, 2, share, hidden),
+            flops,
+            inputs,
+            *weights,
         )
 
-    away = swap_cores(terms(inputs[N_NEAR // 2 :]))
-    share = half // QUAD
-    summed = (terms(inputs[: N_NEAR // 2]) + away).reshape(2, QUAD, share, hidden)
-    preact, act_grad = jnp.sum(exchange(summed.transpose(1, 0, 2, 3), "y", QUADS), axis=0)
+    summed = swap_cores(terms(N_NEAR // 2))
+    summed = terms(0) + summed
+    preact, act_grad = jnp.sum(exchange(summed, "y", QUADS), axis=0)
     act_cdf = 0.5 * (1.0 + jax.scipy.special.erf(preact / math.sqrt(2.0)))
     activated = preact * act_cdf
     pre_grad = act_grad * (
@@ -119,25 +209,14 @@
     own = exchange(copies(jnp.stack([activated, pre_grad]), QUAD), "y", QUADS)
     other = swap_cores(own)
 
-    def results(both):
-        active, pregrad = (both[:, k].reshape(half, hidden) for k in range(2))
-        return jnp.stack(
-            [
-                jnp.stack(
-                    [
-                        product(active, reduce[p], ((1,), (0,))),
-                        product(pregrad, expand[p], ((1,), (1,))),
-                    ]
-                ).reshape(2, N_NEAR // 2, rows, width)
-                for p in range(2)
-            ]
-        )
-
-    outs = jnp.concatenate([results(own), results(other)], axis=2)
-    outs = outs.transpose(2, 0, 1, 3, 4)
+    tail = (2, 2, rows, width)
+    outs = local_call(
+        functools.partial(results_kernel, None), (N_NEAR // 2, *tail), flops, own, *weights
+    )
+    outs = local_call(results_kernel, (N_NEAR, *tail), flops, outs, other, *weights)
     outs, own, other = lax.optimization_barrier((outs, own, other))
-    near = jnp.sum(exchange(outs, CELL, BLOCKS), axis=0)
-    near = own_first(near).reshape(2, 2, N_FAR, part, width).transpose(2, 0, 1, 3, 4)
+    near = exchange(outs, CELL, BLOCKS)
+    near = local_call(fold_kernel, (N_FAR, 2, 2, part, width), near.size, odd, near)
 
     flat = [
         jnp.concatenate([own[:, k].reshape(half, hidden), other[:, k].reshape(half, hidden)])

time: 144 us -> 142 us (0.986)
  matrix products: 16.3 us -> 5.83 us
  Pallas kernels: 0 us -> 6.13 us
  local copies, waits for them, and re-layouts: 6.38 us -> 8.49 us
    ppermute x3, waiting for transfers between devices: 4.23 us -> 21.1 us  [swap_pair(): return lax.ppermute(block, ('y', 'core'), PARTNERS)]
    all_to_all x4, waiting for transfers between devices: 28.8 us -> 12.5 us  [exchange(): lax.all_to_all(blocks, axis, split_axis=0, concat_axis=0, tiled=True, axi...]
    dot_general x20 -> x4, matrix products: 16.3 us -> 5.83 us  [product(): lax.dot_general(left, right, (dims, ((), ())), precision=precise, preferr...]
    unnamed x14 -> x28, local copies, waits for them, and re-layouts: 0.4 us -> 6.92 us
    pallas_call x0 -> x7, Pallas kernels: none -> 6.13 us  [local_call(): pl.pallas_call(kernel, out_shape=jax.ShapeDtypeStruct(shape, jnp.float32)...]
    broadcast_in_dim x3 -> x1, local copies, waits for them, and re-layouts: 2.14 us -> 0.03 us  [copies(): return jnp.broadcast_to(block[None], (count, *block.shape))]
  transfers between devices with their start and end apart: 9 -> 9, of which waited for: 5 -> 8; matrix products, arithmetic and copies ran while one was open for 10% -> 6% of each run, Pallas kernels for 0% -> 2%
where the time goes in v4:
time: 142 us; the launch traced here: 141 us
  starting transfers between devices  53.2 us (37%)
  waiting for transfers between devices  34.4 us (24%)
  blocking collectives  29.4 us (21%)
  local copies, waits for them, and re-layouts  8.49 us (6%)
  Pallas kernels  6.13 us (4%)
  matrix products  5.83 us (4%)
  other arithmetic  2.25 us (2%)
    all_to_all x4, starting transfers between devices, exchange(): lax.all_to_all(blocks, axis, split_axis=0, concat_axis=0, tiled=True, axi...  31.4 us
    all_to_all x2, blocking collectives, exchange(): lax.all_to_all(blocks, axis, split_axis=0, concat_axis=0, tiled=True, axi...  29.4 us
    ppermute x3, waiting for transfers between devices, swap_pair(): return lax.ppermute(block, ('y', 'core'), PARTNERS)  21.1 us
    ppermute x3, starting transfers between devices, swap_pair(): return lax.ppermute(block, ('y', 'core'), PARTNERS)  12.8 us
    all_to_all x4, waiting for transfers between devices, exchange(): lax.all_to_all(blocks, axis, split_axis=0, concat_axis=0, tiled=True, axi...  12.5 us
    ppermute x2, starting transfers between devices, swap_cores(): return lax.ppermute(block, 'core', [(0, 1), (1, 0)])  9.01 us
    unnamed x28, local copies, waits for them, and re-layouts  6.92 us
    pallas_call x7, Pallas kernels, local_call(): pl.pallas_call(kernel, out_shape=jax.ShapeDtypeStruct(shape, jnp.float32)...  6.13 us
  transfers between devices with their start and end apart: 9, of which 8 were waited for; matrix products, arithmetic and copies ran while one was open for 6% of the time, Pallas kernels for 2%

profile of v4, /device:TPU:1, one launch (start us, length us, event | category | flops | bytes accessed | tf_op | source)
XLA Modules:
  0.0 140.6 jit_solution(16788149508573017879)
XLA Ops:
  0.6 0.0 copy-start
  0.6 0.0 copy-start.11
  0.7 0.8 copy-done.11
  1.4 0.7 copy-done.12
  2.2 0.8 shard_map.75
  3.0 16.3 %all-to-all-start = ((f32[16,2,8,384]{3,2,1,0:T(8,128)}), f32[16,2,8,384]{3,2,1,0:T(8,128)S(1)}, u32[]{:S(2)}, u32[]{:S(2)}) async-start(f32[16,2,8,384]{3,2,1,0:T(8,128)} %bitcast.1), calls=%async_computation | async-start | bytes 786432 | tf_op jit(solution)/shard_map/all_to_all | solution.py:161
  19.3 4.5 %collective-permute-start = (f32[384,384]{1,0:T(8,128)S(1)}, f32[384,384]{1,0:T(8,128)S(1)}, u32[]{:S(2)}, u32[]{:S(2)}) collective-permute-start(f32[384,384]{1,0:T(8,128)S(1)} %copy-done), channel_id=1, source_target_pairs={{0,64},{64,0},{128,192},{192,128},{256,320},{320,256},{384,448},{4... | collective-permute-start | bytes 1769480 | tf_op jit(solution)/shard_map/ppermute | solution.py:157
  23.8 7.9 %collective-permute-done.expand_far = f32[384,384]{1,0:T(8,128)S(1)} collective-permute-done((f32[384,384]{1,0:T(8,128)S(1)}, f32[384,384]{1,0:T(8,128)S(1)}, u32[]{:S(2)}, u32[]{:S(2)}) %collective-permute-start) | collective-permute-done | bytes 589856 | tf_op jit(solution)/shard_map/ppermute | solution.py:157
  31.7 2.6 %all-to-all-done = f32[16,2,8,384]{3,2,1,0:T(8,128)S(1)} async-done(((f32[16,2,8,384]{3,2,1,0:T(8,128)}), f32[16,2,8,384]{3,2,1,0:T(8,128)S(1)}, u32[]{:S(2)}, u32[]{:S(2)}) %all-to-all-start) | async-done | bytes 393248 | tf_op jit(solution)/shard_map/all_to_all | solution.py:161
  34.4 0.1 shard_map.76
  34.5 1.2 copy-done.5
  35.6 5.5 %all-to-all-start.1 = ((f32[4,2,2,64,384]{4,3,2,1,0:T(8,128)}), f32[4,2,2,64,384]{4,3,2,1,0:T(8,128)S(1)}, u32[]{:S(2)}, u32[]{:S(2)}) async-start(f32[4,2,2,64,384]{4,3,2,1,0:T(8,128)} %copy-done.5), calls=%async_computation.1 | async-start | bytes 3145728 | tf_op jit(solution)/shard_map/all_to_all | solution.py:161
  41.1 5.6 %collective-permute-start.1 = (f32[384,384]{1,0:T(8,128)S(1)}, f32[384,384]{1,0:T(8,128)S(1)}, u32[]{:S(2)}, u32[]{:S(2)}) collective-permute-start(f32[384,384]{1,0:T(8,128)S(1)} %copy-done.1), channel_id=1, source_target_pairs={{0,64},{64,0},{128,192},{192,128},{256,320},{320,256},{384,448},{4... | collective-permute-start | bytes 1769480 | tf_op jit(solution)/shard_map/ppermute | solution.py:157
  46.7 7.3 %collective-permute-done.1.reduce_far = f32[384,384]{1,0:T(8,128)S(1)} collective-permute-done((f32[384,384]{1,0:T(8,128)S(1)}, f32[384,384]{1,0:T(8,128)S(1)}, u32[]{:S(2)}, u32[]{:S(2)}) %collective-permute-start.1) | collective-permute-done | bytes 589856 | tf_op jit(solution)/shard_map/ppermute | solution.py:157
  54.0 0.8 copy-done.2
  54.8 0.0 all-to-all-done.1.inputs
  54.8 1.1 copy-done.3
  55.9 1.1 shard_map.78
  57.0 1.9 %collective-permute-start.2 = (f32[4,2,32,384]{3,2,1,0:T(8,128)S(1)}, f32[4,2,32,384]{3,2,1,0:T(8,128)S(1)}, u32[]{:S(2)}, u32[]{:S(2)}) collective-permute-start(f32[4,2,32,384]{3,2,1,0:T(8,128)S(1)} %shard_map.78), channel_id=1, source_target_pairs={{0,32},{32,0},{1,33},{33,1},{2,34},{34,2},{3,35},{35,3},{4,36},{36... | collective-permute-start | bytes 1179656 | tf_op jit(solution)/shard_map/ppermute | solution.py:153
  58.9 1.1 shard_map.77
  60.0 0.6 collective-permute-done.2
  60.6 15.2 %all_to_all.30 = f32[4,2,32,384]{3,2,1,0:T(8,128)} all-to-all(f32[4,2,32,384]{3,2,1,0:T(8,128)S(1)} %add.26), channel_id=1, replica_groups={{0,128,256,384},{64,192,320,448},{1,129,257,385},{65,193,321,449},{2,13..., dimensions={0} | all-to-all | bytes 786432 | tf_op jit(solution)/shard_map/all_to_all | solution.py:161
  75.8 1.0 reduce_sum.18
  76.8 0.0 copy-start.4
  76.9 14.3 %all_to_all.31.both = f32[4,2,32,384]{3,2,1,0:T(8,128)S(1)} all-to-all(f32[4,2,32,384]{3,2,1,0:T(8,128)S(1)} %broadcast_in_dim.2), channel_id=1, replica_groups={{0,128,256,384},{64,192,320,448},{1,129,257,385},{65,193,321,449},{2,13..., dimensions={0} | all-to-all | bytes 786432 | tf_op jit(solution)/shard_map/all_to_all | solution.py:161
  91.2 7.1 %collective-permute-start.3 = (f32[4,2,32,384]{3,2,1,0:T(8,128)S(1)}, f32[4,2,32,384]{3,2,1,0:T(8,128)S(1)}, u32[]{:S(2)}, u32[]{:S(2)}) collective-permute-start(f32[4,2,32,384]{3,2,1,0:T(8,128)S(1)} %all_to_all.31.both), channel_id=1, source_target_pairs={{0,32},{32,0},{1,33},{33,1},{2,34},{34,2},{3,35},{35,3},{4,36},{36... | collective-permute-start | bytes 1179656 | tf_op jit(solution)/shard_map/ppermute | solution.py:153
  98.3 1.1 shard_map.79.earlier
  99.4 0.2 collective-permute-done.3.both
  99.6 1.2 shard_map.80
  100.8 1.2 copy-done.6
  102.0 0.8 copy-done.9
  102.7 6.1 %all-to-all-start.4 = ((f32[4,2,2,64,384]{4,3,2,1,0:T(8,128)}), f32[4,2,2,64,384]{4,3,2,1,0:T(8,128)S(1)}, u32[]{:S(2)}, u32[]{:S(2)}) async-start(f32[4,2,2,64,384]{4,3,2,1,0:T(8,128)} %copy-done.6), calls=%async_computation.4 | async-start | bytes 3145728 | tf_op jit(solution)/shard_map/all_to_all | solution.py:161
  108.8 0.9 fusion.13
  109.7 0.1 copy-done.8
  109.8 0.3 copy-done.10
  110.1 0.1 fusion.14
  110.1 0.5 convolution_bitcast_fusion
  110.7 0.5 convolution_bitcast_fusion.1
  111.2 1.1 pad_maximum_fusion
  112.3 2.7 %collective-permute-start.4 = (f32[2,384,384]{2,1,0:T(8,128)}, f32[2,384,384]{2,1,0:T(8,128)}, u32[]{:S(2)}, u32[]{:S(2)}) collective-permute-start(f32[2,384,384]{2,1,0:T(8,128)} %pad_maximum_fusion), channel_id=1, source_target_pairs={{0,64},{64,0},{128,192},{192,128},{256,320},{320,256},{384,448},{4... | collective-permute-start | bytes 3538952 | tf_op jit(solution)/shard_map/ppermute | solution.py:157
  115.0 5.8 %all-to-all-done.4.near = f32[4,2,2,64,384]{4,3,2,1,0:T(8,128)S(1)} async-done(((f32[4,2,2,64,384]{4,3,2,1,0:T(8,128)}), f32[4,2,2,64,384]{4,3,2,1,0:T(8,128)S(1)}, u32[]{:S(2)}, u32[]{:S(2)}) %all-to-all-start.4) | async-done | bytes 1572896 | tf_op jit(solution)/shard_map/all_to_all | solution.py:161
  120.8 0.8 shard_map.81
  121.6 3.6 %all-to-all-start.5 = ((f32[16,2,8,384]{3,2,1,0:T(8,128)}), f32[16,2,8,384]{3,2,1,0:T(8,128)S(1)}, u32[]{:S(2)}, u32[]{:S(2)}) async-start(f32[16,2,8,384]{3,2,1,0:T(8,128)} %bitcast.3), calls=%async_computation.5 | async-start | bytes 786432 | tf_op jit(solution)/shard_map/all_to_all | solution.py:161
  125.2 5.9 %collective-permute-done.4 = f32[2,384,384]{2,1,0:T(8,128)} collective-permute-done((f32[2,384,384]{2,1,0:T(8,128)}, f32[2,384,384]{2,1,0:T(8,128)}, u32[]{:S(2)}, u32[]{:S(2)}) %collective-permute-start.4) | collective-permute-done | bytes 1179680 | tf_op jit(solution)/shard_map/ppermute | solution.py:157
  131.1 2.4 %fusion = f32[384,384]{1,0:T(8,128)} fusion(f32[2,384,384]{2,1,0:T(8,128)} %collective-permute-done.4, f32[256,384]{1,0:T(8,128)S(1)} %bitcast.46, f32[128,384]{1,0:T(8,128)S(1)} %bitcast.41, f32[128,384]{1,0:T(8,128)S(1)} %bitcast.39), kind=kOutput, calls=%fused_computation.4 | convolution fusion | flops 226738176 | bytes 1966080 | tf_op jit(solution)/shard_map/dot_general | solution.py:55
  133.5 2.4 %fusion.1 = f32[384,384]{1,0:T(8,128)} fusion(f32[2,384,384]{2,1,0:T(8,128)} %collective-permute-done.4, f32[256,384]{1,0:T(8,128)S(1)} %bitcast.45, f32[128,384]{1,0:T(8,128)S(1)} %bitcast.37, f32[128,384]{1,0:T(8,128)S(1)} %bitcast.35), kind=kOutput, calls=%fused_computation.6 | convolution fusion | flops 226738176 | bytes 1966080 | tf_op jit(solution)/shard_map/dot_general | solution.py:55
  135.9 4.1 %all-to-all-done.5 = f32[16,2,8,384]{3,2,1,0:T(8,128)S(1)} async-done(((f32[16,2,8,384]{3,2,1,0:T(8,128)}), f32[16,2,8,384]{3,2,1,0:T(8,128)S(1)}, u32[]{:S(2)}, u32[]{:S(2)}) %all-to-all-start.5) | async-done | bytes 393248 | tf_op jit(solution)/shard_map/all_to_all | solution.py:161
  140.0 0.6 slice_bitcast_fusion.2
  (21 shorter events, 0.2 us)
Async XLA Ops:
  0.6 18.7 %copy-start = (f32[384,384]{1,0:T(8,128)S(1)}, f32[384,384]{1,0:T(8,128)}, u32[]{:S(2)}) copy-start(f32[384,384]{1,0:T(8,128)} %expand.7) | copy-start | bytes 1769476
  0.6 0.8 copy-start.11
  1.4 0.7 copy-start.12
  3.0 31.4 %all-to-all-start = ((f32[16,2,8,384]{3,2,1,0:T(8,128)}), f32[16,2,8,384]{3,2,1,0:T(8,128)S(1)}, u32[]{:S(2)}, u32[]{:S(2)}) async-start(f32[16,2,8,384]{3,2,1,0:T(8,128)} %bitcast.1), calls=%async_computation | async-start | bytes 786432 | tf_op jit(solution)/shard_map/all_to_all | solution.py:161
  19.3 12.4 %collective-permute-start = (f32[384,384]{1,0:T(8,128)S(1)}, f32[384,384]{1,0:T(8,128)S(1)}, u32[]{:S(2)}, u32[]{:S(2)}) collective-permute-start(f32[384,384]{1,0:T(8,128)S(1)} %copy-done), channel_id=1, source_target_pairs={{0,64},{64,0},{128,192},{192,128},{256,320},{320,256},{384,448},{4... | collective-permute-start | bytes 1769480 | tf_op jit(solution)/shard_map/ppermute | solution.py:157
  34.5 1.2 copy-start.5
  35.6 5.5 %copy-start.1 = (f32[384,384]{1,0:T(8,128)S(1)}, f32[384,384]{1,0:T(8,128)}, u32[]{:S(2)}) copy-start(f32[384,384]{1,0:T(8,128)} %reduce.7) | copy-start | bytes 1769476
  35.6 19.2 %all-to-all-start.1 = ((f32[4,2,2,64,384]{4,3,2,1,0:T(8,128)}), f32[4,2,2,64,384]{4,3,2,1,0:T(8,128)S(1)}, u32[]{:S(2)}, u32[]{:S(2)}) async-start(f32[4,2,2,64,384]{4,3,2,1,0:T(8,128)} %copy-done.5), calls=%async_computation.1 | async-start | bytes 3145728 | tf_op jit(solution)/shard_map/all_to_all | solution.py:161
  41.1 12.8 %collective-permute-start.1 = (f32[384,384]{1,0:T(8,128)S(1)}, f32[384,384]{1,0:T(8,128)S(1)}, u32[]{:S(2)}, u32[]{:S(2)}) collective-permute-start(f32[384,384]{1,0:T(8,128)S(1)} %copy-done.1), channel_id=1, source_target_pairs={{0,64},{64,0},{128,192},{192,128},{256,320},{320,256},{384,448},{4... | collective-permute-start | bytes 1769480 | tf_op jit(solution)/shard_map/ppermute | solution.py:157
  54.0 0.8 copy-start.2
  54.8 1.1 copy-start.3
  57.0 3.6 %collective-permute-start.2 = (f32[4,2,32,384]{3,2,1,0:T(8,128)S(1)}, f32[4,2,32,384]{3,2,1,0:T(8,128)S(1)}, u32[]{:S(2)}, u32[]{:S(2)}) collective-permute-start(f32[4,2,32,384]{3,2,1,0:T(8,128)S(1)} %shard_map.78), channel_id=1, source_target_pairs={{0,32},{32,0},{1,33},{33,1},{2,34},{34,2},{3,35},{35,3},{4,36},{36... | collective-permute-start | bytes 1179656 | tf_op jit(solution)/shard_map/ppermute | solution.py:153
  76.8 21.5 %copy-start.4 = (f32[384,384]{1,0:T(8,128)S(1)}, f32[384,384]{1,0:T(8,128)}, u32[]{:S(2)}) copy-start(f32[384,384]{1,0:T(8,128)} %copy-done.2) | copy-start | bytes 1769476
  91.2 8.2 %copy-start.7 = (f32[4,2,32,384]{3,2,1,0:T(8,128)}, f32[4,2,32,384]{3,2,1,0:T(8,128)S(1)}, u32[]{:S(2)}) copy-start(f32[4,2,32,384]{3,2,1,0:T(8,128)S(1)} %all_to_all.31.both) | copy-start | bytes 1179652
  91.2 8.4 %collective-permute-start.3 = (f32[4,2,32,384]{3,2,1,0:T(8,128)S(1)}, f32[4,2,32,384]{3,2,1,0:T(8,128)S(1)}, u32[]{:S(2)}, u32[]{:S(2)}) collective-permute-start(f32[4,2,32,384]{3,2,1,0:T(8,128)S(1)} %all_to_all.31.both), channel_id=1, source_target_pairs={{0,32},{32,0},{1,33},{33,1},{2,34},{34,2},{3,35},{35,3},{4,36},{36... | collective-permute-start | bytes 1179656 | tf_op jit(solution)/shard_map/ppermute | solution.py:153
  100.8 1.2 copy-start.6
  102.0 0.8 copy-start.9
  102.7 18.0 %all-to-all-start.4 = ((f32[4,2,2,64,384]{4,3,2,1,0:T(8,128)}), f32[4,2,2,64,384]{4,3,2,1,0:T(8,128)S(1)}, u32[]{:S(2)}, u32[]{:S(2)}) async-start(f32[4,2,2,64,384]{4,3,2,1,0:T(8,128)} %copy-done.6), calls=%async_computation.4 | async-start | bytes 3145728 | tf_op jit(solution)/shard_map/all_to_all | solution.py:161
  108.8 1.0 copy-start.8
  108.8 1.3 copy-start.10
  112.3 18.8 %copy-start.13 = (f32[4,1,1,64,384]{4,3,2,1,0:T(8,128)S(1)}, f32[4,1,1,64,384]{4,3,2,1,0:T(8,128)}, u32[]{:S(2)}) copy-start(f32[4,1,1,64,384]{4,3,2,1,0:T(8,128)} %get-tuple-element.14) | copy-start | bytes 1179652
  112.3 18.8 %collective-permute-start.4 = (f32[2,384,384]{2,1,0:T(8,128)}, f32[2,384,384]{2,1,0:T(8,128)}, u32[]{:S(2)}, u32[]{:S(2)}) collective-permute-start(f32[2,384,384]{2,1,0:T(8,128)} %pad_maximum_fusion), channel_id=1, source_target_pairs={{0,64},{64,0},{128,192},{192,128},{256,320},{320,256},{384,448},{4... | collective-permute-start | bytes 3538952 | tf_op jit(solution)/shard_map/ppermute | solution.py:157
  121.6 18.4 %all-to-all-start.5 = ((f32[16,2,8,384]{3,2,1,0:T(8,128)}), f32[16,2,8,384]{3,2,1,0:T(8,128)S(1)}, u32[]{:S(2)}, u32[]{:S(2)}) async-start(f32[16,2,8,384]{3,2,1,0:T(8,128)} %bitcast.3), calls=%async_computation.5 | async-start | bytes 786432 | tf_op jit(solution)/shard_map/all_to_all | solution.py:161

commit v5 on v4

--- a/solution.py
+++ b/solution.py
@@ -98,15 +98,6 @@
             term = product_of_halves(block, halves(weights[array][pair][...]), array == 1)
             for n in range(2):
                 out[at + n, pair, array] = term[n * rows : (n + 1) * rows]
-
-
-def send_kernel(patches, cotangent, out):
-    part = out.shape[3]
-    for p in range(2):
-        for array, source in enumerate((patches, cotangent)):
-            block = source[p * part : (p + 1) * part]
-            for m in range(N_FAR):
-                out[m, p, array] = block
 
 
 def spread_kernel(odd, far, out):
@@ -174,8 +165,8 @@
     part = tokens // 2
     rows = N_FAR * part
 
-    mine = local_call(send_kernel, (N_FAR, 2, 2, part, width), 0, patches, cotangent)
-    far = exchange(mine.reshape(2 * N_FAR, 2, part, width), ALL, FAR)
+    mine = jnp.stack([patches.reshape(2, part, width), cotangent.reshape(2, part, width)], axis=1)
+    far = exchange(copies(mine, N_FAR).reshape(2 * N_FAR, 2, part, width), ALL, FAR)
     far = far.reshape(N_FAR, 2, 2, part, width)
     far, other_expand = lax.optimization_barrier((far, swap_pair(expand_weight)))
     inputs = local_call(spread_kernel, (N_NEAR, 2, 2, rows, width), 0, odd, far)
@@ -214,7 +205,6 @@
         functools.partial(results_kernel, None), (N_NEAR // 2, *tail), flops, own, *weights
     )
     outs = local_call(results_kernel, (N_NEAR, *tail), flops, outs, other, *weights)
-    outs, own, other = lax.optimization_barrier((outs, own, other))
     near = exchange(outs, CELL, BLOCKS)
     near = local_call(fold_kernel, (N_FAR, 2, 2, part, width), near.size, odd, near)
 

time: 142 us -> 141 us (level)
    unnamed x28 -> x24, local copies, waits for them, and re-layouts: 6.92 us -> 5.28 us
    pallas_call x7 -> x6, Pallas kernels: 6.13 us -> 5.37 us  [local_call(): pl.pallas_call(kernel, out_shape=jax.ShapeDtypeStruct(shape, jnp.float32)...]
where the time goes in v5:
time: 141 us; the launch traced here: 140 us
  starting transfers between devices  53.2 us (38%)
  waiting for transfers between devices  34.5 us (24%)
  blocking collectives  29.4 us (21%)
  local copies, waits for them, and re-layouts  7.65 us (5%)
  matrix products  5.84 us (4%)
  Pallas kernels  5.37 us (4%)
  other arithmetic  3.07 us (2%)
    all_to_all x4, starting transfers between devices, exchange(): lax.all_to_all(blocks, axis, split_axis=0, concat_axis=0, tiled=True, axi...  31.4 us
    all_to_all x2, blocking collectives, exchange(): lax.all_to_all(blocks, axis, split_axis=0, concat_axis=0, tiled=True, axi...  29.4 us
    ppermute x3, waiting for transfers between devices, swap_pair(): return lax.ppermute(block, ('y', 'core'), PARTNERS)  20.9 us
    ppermute x3, starting transfers between devices, swap_pair(): return lax.ppermute(block, ('y', 'core'), PARTNERS)  12.8 us
    all_to_all x4, waiting for transfers between devices, exchange(): lax.all_to_all(blocks, axis, split_axis=0, concat_axis=0, tiled=True, axi...  12.8 us
    ppermute x2, starting transfers between devices, swap_cores(): return lax.ppermute(block, 'core', [(0, 1), (1, 0)])  9.01 us
    dot_general x4, matrix products, product(): lax.dot_general(left, right, (dims, ((), ())), precision=precise, preferr...  5.84 us
    pallas_call x6, Pallas kernels, local_call(): pl.pallas_call(kernel, out_shape=jax.ShapeDtypeStruct(shape, jnp.float32)...  5.37 us
  transfers between devices with their start and end apart: 9, of which 8 were waited for; matrix products, arithmetic and copies ran while one was open for 6% of the time, Pallas kernels for 2%

profile of v5, /device:TPU:1, one launch (start us, length us, event | category | flops | bytes accessed | tf_op | source)
XLA Modules:
  0.0 139.9 jit_solution(11365387915969029373)
XLA Ops:
  0.6 0.0 copy-start
  0.6 0.8 pad_maximum_fusion.8
  1.5 0.8 broadcast_in_dim.4
  2.2 16.3 %all-to-all-start = ((f32[16,2,8,384]{3,2,1,0:T(8,128)}), f32[16,2,8,384]{3,2,1,0:T(8,128)S(1)}, u32[]{:S(2)}, u32[]{:S(2)}) async-start(f32[16,2,8,384]{3,2,1,0:T(8,128)} %bitcast.3), calls=%async_computation | async-start | bytes 786432 | tf_op jit(solution)/shard_map/all_to_all | solution.py:152
  18.6 0.0 copy-done
  18.6 4.5 %collective-permute-start = (f32[384,384]{1,0:T(8,128)S(1)}, f32[384,384]{1,0:T(8,128)S(1)}, u32[]{:S(2)}, u32[]{:S(2)}) collective-permute-start(f32[384,384]{1,0:T(8,128)S(1)} %copy-done), channel_id=1, source_target_pairs={{0,64},{64,0},{128,192},{192,128},{256,320},{320,256},{384,448},{4... | collective-permute-start | bytes 1769480 | tf_op jit(solution)/shard_map/ppermute | solution.py:148
  23.1 7.9 %collective-permute-done.expand_far = f32[384,384]{1,0:T(8,128)S(1)} collective-permute-done((f32[384,384]{1,0:T(8,128)S(1)}, f32[384,384]{1,0:T(8,128)S(1)}, u32[]{:S(2)}, u32[]{:S(2)}) %collective-permute-start) | collective-permute-done | bytes 589856 | tf_op jit(solution)/shard_map/ppermute | solution.py:148
  31.0 2.6 %all-to-all-done = f32[16,2,8,384]{3,2,1,0:T(8,128)S(1)} async-done(((f32[16,2,8,384]{3,2,1,0:T(8,128)}), f32[16,2,8,384]{3,2,1,0:T(8,128)S(1)}, u32[]{:S(2)}, u32[]{:S(2)}) %all-to-all-start) | async-done | bytes 393248 | tf_op jit(solution)/shard_map/all_to_all | solution.py:152
  33.7 0.1 shard_map.75
  33.8 0.0 copy-start.5
  33.8 1.1 copy-done.5
  34.9 5.5 %all-to-all-start.1 = ((f32[4,2,2,64,384]{4,3,2,1,0:T(8,128)}), f32[4,2,2,64,384]{4,3,2,1,0:T(8,128)S(1)}, u32[]{:S(2)}, u32[]{:S(2)}) async-start(f32[4,2,2,64,384]{4,3,2,1,0:T(8,128)} %copy-done.5), calls=%async_computation.1 | async-start | bytes 3145728 | tf_op jit(solution)/shard_map/all_to_all | solution.py:152
  40.4 0.0 copy-done.1
  40.4 5.6 %collective-permute-start.1 = (f32[384,384]{1,0:T(8,128)S(1)}, f32[384,384]{1,0:T(8,128)S(1)}, u32[]{:S(2)}, u32[]{:S(2)}) collective-permute-start(f32[384,384]{1,0:T(8,128)S(1)} %copy-done.1), channel_id=1, source_target_pairs={{0,64},{64,0},{128,192},{192,128},{256,320},{320,256},{384,448},{4... | collective-permute-start | bytes 1769480 | tf_op jit(solution)/shard_map/ppermute | solution.py:148
  46.0 7.3 %collective-permute-done.1.reduce_far = f32[384,384]{1,0:T(8,128)S(1)} collective-permute-done((f32[384,384]{1,0:T(8,128)S(1)}, f32[384,384]{1,0:T(8,128)S(1)}, u32[]{:S(2)}, u32[]{:S(2)}) %collective-permute-start.1) | collective-permute-done | bytes 589856 | tf_op jit(solution)/shard_map/ppermute | solution.py:148
  53.3 0.8 copy-done.2
  54.1 0.0 all-to-all-done.1.inputs
  54.1 1.1 copy-done.3
  55.2 1.1 shard_map.77
  56.2 1.9 %collective-permute-start.2 = (f32[4,2,32,384]{3,2,1,0:T(8,128)S(1)}, f32[4,2,32,384]{3,2,1,0:T(8,128)S(1)}, u32[]{:S(2)}, u32[]{:S(2)}) collective-permute-start(f32[4,2,32,384]{3,2,1,0:T(8,128)S(1)} %shard_map.77), channel_id=1, source_target_pairs={{0,32},{32,0},{1,33},{33,1},{2,34},{34,2},{3,35},{35,3},{4,36},{36... | collective-permute-start | bytes 1179656 | tf_op jit(solution)/shard_map/ppermute | solution.py:144
  58.2 1.1 shard_map.76
  59.3 0.6 collective-permute-done.2
  59.9 15.2 %all_to_all.30 = f32[4,2,32,384]{3,2,1,0:T(8,128)} all-to-all(f32[4,2,32,384]{3,2,1,0:T(8,128)S(1)} %add.26), channel_id=1, replica_groups={{0,128,256,384},{64,192,320,448},{1,129,257,385},{65,193,321,449},{2,13..., dimensions={0} | all-to-all | bytes 786432 | tf_op jit(solution)/shard_map/all_to_all | solution.py:152
  75.1 1.0 reduce_sum.18
  76.1 0.0 copy-start.4
  76.2 14.3 %all_to_all.31.both = f32[4,2,32,384]{3,2,1,0:T(8,128)S(1)} all-to-all(f32[4,2,32,384]{3,2,1,0:T(8,128)S(1)} %broadcast_in_dim.5), channel_id=1, replica_groups={{0,128,256,384},{64,192,320,448},{1,129,257,385},{65,193,321,449},{2,13..., dimensions={0} | all-to-all | bytes 786432 | tf_op jit(solution)/shard_map/all_to_all | solution.py:152
  90.5 7.1 %collective-permute-start.3 = (f32[4,2,32,384]{3,2,1,0:T(8,128)S(1)}, f32[4,2,32,384]{3,2,1,0:T(8,128)S(1)}, u32[]{:S(2)}, u32[]{:S(2)}) collective-permute-start(f32[4,2,32,384]{3,2,1,0:T(8,128)S(1)} %all_to_all.31.both), channel_id=1, source_target_pairs={{0,32},{32,0},{1,33},{33,1},{2,34},{34,2},{3,35},{35,3},{4,36},{36... | collective-permute-start | bytes 1179656 | tf_op jit(solution)/shard_map/ppermute | solution.py:144
  97.6 1.1 shard_map.78.earlier
  98.7 0.2 collective-permute-done.3.both
  98.9 1.2 shard_map.79
  100.1 1.1 copy-done.6
  101.2 0.7 copy-done.9
  102.0 6.1 %all-to-all-start.4 = ((f32[4,2,2,64,384]{4,3,2,1,0:T(8,128)}), f32[4,2,2,64,384]{4,3,2,1,0:T(8,128)S(1)}, u32[]{:S(2)}, u32[]{:S(2)}) async-start(f32[4,2,2,64,384]{4,3,2,1,0:T(8,128)} %copy-done.6), calls=%async_computation.4 | async-start | bytes 3145728 | tf_op jit(solution)/shard_map/all_to_all | solution.py:152
  108.0 0.9 fusion.9
  108.9 0.1 copy-done.8
  109.1 0.2 copy-done.10
  109.3 0.5 convolution_bitcast_fusion
  109.9 0.5 convolution_bitcast_fusion.1
  110.4 1.1 pad_maximum_fusion
  111.5 2.7 %collective-permute-start.4 = (f32[2,384,384]{2,1,0:T(8,128)}, f32[2,384,384]{2,1,0:T(8,128)}, u32[]{:S(2)}, u32[]{:S(2)}) collective-permute-start(f32[2,384,384]{2,1,0:T(8,128)} %pad_maximum_fusion), channel_id=1, source_target_pairs={{0,64},{64,0},{128,192},{192,128},{256,320},{320,256},{384,448},{4... | collective-permute-start | bytes 3538952 | tf_op jit(solution)/shard_map/ppermute | solution.py:148
  114.2 5.8 %all-to-all-done.4.near = f32[4,2,2,64,384]{4,3,2,1,0:T(8,128)S(1)} async-done(((f32[4,2,2,64,384]{4,3,2,1,0:T(8,128)}), f32[4,2,2,64,384]{4,3,2,1,0:T(8,128)S(1)}, u32[]{:S(2)}, u32[]{:S(2)}) %all-to-all-start.4) | async-done | bytes 1572896 | tf_op jit(solution)/shard_map/all_to_all | solution.py:152
  120.0 0.8 shard_map.80
  120.8 3.6 %all-to-all-start.5 = ((f32[16,2,8,384]{3,2,1,0:T(8,128)}), f32[16,2,8,384]{3,2,1,0:T(8,128)S(1)}, u32[]{:S(2)}, u32[]{:S(2)}) async-start(f32[16,2,8,384]{3,2,1,0:T(8,128)} %bitcast.5), calls=%async_computation.5 | async-start | bytes 786432 | tf_op jit(solution)/shard_map/all_to_all | solution.py:152
  124.4 5.7 %collective-permute-done.4 = f32[2,384,384]{2,1,0:T(8,128)} collective-permute-done((f32[2,384,384]{2,1,0:T(8,128)}, f32[2,384,384]{2,1,0:T(8,128)}, u32[]{:S(2)}, u32[]{:S(2)}) %collective-permute-start.4) | collective-permute-done | bytes 1179680 | tf_op jit(solution)/shard_map/ppermute | solution.py:148
  130.1 2.4 %convolution_add_fusion.1 = f32[384,384]{1,0:T(8,128)} fusion(f32[256,384]{1,0:T(8,128)S(1)} %bitcast.48, f32[2,384,384]{2,1,0:T(8,128)} %collective-permute-done.4, f32[128,384]{1,0:T(8,128)S(1)} %bitcast.43, f32[128,384]{1,0:T(8,128)S(1)} %bitcast.41), kind=kOutput, calls=%fused_computation.3 | convolution fusion | flops 226738176 | bytes 1966080 | tf_op jit(solution)/shard_map/dot_general | solution.py:55
  132.5 2.4 %convolution_add_fusion = f32[384,384]{1,0:T(8,128)} fusion(f32[256,384]{1,0:T(8,128)S(1)} %bitcast.47, f32[2,384,384]{2,1,0:T(8,128)} %collective-permute-done.4, f32[128,384]{1,0:T(8,128)S(1)} %bitcast.39, f32[128,384]{1,0:T(8,128)S(1)} %bitcast.37), kind=kOutput, calls=%fused_computation | convolution fusion | flops 226738176 | bytes 1966080 | tf_op jit(solution)/shard_map/dot_general | solution.py:55
  134.9 4.3 %all-to-all-done.5 = f32[16,2,8,384]{3,2,1,0:T(8,128)S(1)} async-done(((f32[16,2,8,384]{3,2,1,0:T(8,128)}), f32[16,2,8,384]{3,2,1,0:T(8,128)S(1)}, u32[]{:S(2)}, u32[]{:S(2)}) %all-to-all-start.5) | async-done | bytes 393248 | tf_op jit(solution)/shard_map/all_to_all | solution.py:152
  139.3 0.6 slice_bitcast_fusion.2
  (20 shorter events, 0.2 us)
Async XLA Ops:
  0.6 17.9 %copy-start = (f32[384,384]{1,0:T(8,128)S(1)}, f32[384,384]{1,0:T(8,128)}, u32[]{:S(2)}) copy-start(f32[384,384]{1,0:T(8,128)} %expand.7) | copy-start | bytes 1769476
  2.2 31.4 %all-to-all-start = ((f32[16,2,8,384]{3,2,1,0:T(8,128)}), f32[16,2,8,384]{3,2,1,0:T(8,128)S(1)}, u32[]{:S(2)}, u32[]{:S(2)}) async-start(f32[16,2,8,384]{3,2,1,0:T(8,128)} %bitcast.3), calls=%async_computation | async-start | bytes 786432 | tf_op jit(solution)/shard_map/all_to_all | solution.py:152
  18.6 12.4 %collective-permute-start = (f32[384,384]{1,0:T(8,128)S(1)}, f32[384,384]{1,0:T(8,128)S(1)}, u32[]{:S(2)}, u32[]{:S(2)}) collective-permute-start(f32[384,384]{1,0:T(8,128)S(1)} %copy-done), channel_id=1, source_target_pairs={{0,64},{64,0},{128,192},{192,128},{256,320},{320,256},{384,448},{4... | collective-permute-start | bytes 1769480 | tf_op jit(solution)/shard_map/ppermute | solution.py:148
  33.8 1.2 copy-start.5
  34.9 5.5 %copy-start.1 = (f32[384,384]{1,0:T(8,128)S(1)}, f32[384,384]{1,0:T(8,128)}, u32[]{:S(2)}) copy-start(f32[384,384]{1,0:T(8,128)} %reduce.7) | copy-start | bytes 1769476
  34.9 19.2 %all-to-all-start.1 = ((f32[4,2,2,64,384]{4,3,2,1,0:T(8,128)}), f32[4,2,2,64,384]{4,3,2,1,0:T(8,128)S(1)}, u32[]{:S(2)}, u32[]{:S(2)}) async-start(f32[4,2,2,64,384]{4,3,2,1,0:T(8,128)} %copy-done.5), calls=%async_computation.1 | async-start | bytes 3145728 | tf_op jit(solution)/shard_map/all_to_all | solution.py:152
  40.4 12.8 %collective-permute-start.1 = (f32[384,384]{1,0:T(8,128)S(1)}, f32[384,384]{1,0:T(8,128)S(1)}, u32[]{:S(2)}, u32[]{:S(2)}) collective-permute-start(f32[384,384]{1,0:T(8,128)S(1)} %copy-done.1), channel_id=1, source_target_pairs={{0,64},{64,0},{128,192},{192,128},{256,320},{320,256},{384,448},{4... | collective-permute-start | bytes 1769480 | tf_op jit(solution)/shard_map/ppermute | solution.py:148
  53.3 0.8 copy-start.2
  54.1 1.1 copy-start.3
  56.2 3.6 %collective-permute-start.2 = (f32[4,2,32,384]{3,2,1,0:T(8,128)S(1)}, f32[4,2,32,384]{3,2,1,0:T(8,128)S(1)}, u32[]{:S(2)}, u32[]{:S(2)}) collective-permute-start(f32[4,2,32,384]{3,2,1,0:T(8,128)S(1)} %shard_map.77), channel_id=1, source_target_pairs={{0,32},{32,0},{1,33},{33,1},{2,34},{34,2},{3,35},{35,3},{4,36},{36... | collective-permute-start | bytes 1179656 | tf_op jit(solution)/shard_map/ppermute | solution.py:144
  76.1 21.5 %copy-start.4 = (f32[384,384]{1,0:T(8,128)S(1)}, f32[384,384]{1,0:T(8,128)}, u32[]{:S(2)}) copy-start(f32[384,384]{1,0:T(8,128)} %copy-done.2) | copy-start | bytes 1769476
  90.5 8.2 %copy-start.7 = (f32[4,2,32,384]{3,2,1,0:T(8,128)}, f32[4,2,32,384]{3,2,1,0:T(8,128)S(1)}, u32[]{:S(2)}) copy-start(f32[4,2,32,384]{3,2,1,0:T(8,128)S(1)} %all_to_all.31.both) | copy-start | bytes 1179652
  90.5 8.4 %collective-permute-start.3 = (f32[4,2,32,384]{3,2,1,0:T(8,128)S(1)}, f32[4,2,32,384]{3,2,1,0:T(8,128)S(1)}, u32[]{:S(2)}, u32[]{:S(2)}) collective-permute-start(f32[4,2,32,384]{3,2,1,0:T(8,128)S(1)} %all_to_all.31.both), channel_id=1, source_target_pairs={{0,32},{32,0},{1,33},{33,1},{2,34},{34,2},{3,35},{35,3},{4,36},{36... | collective-permute-start | bytes 1179656 | tf_op jit(solution)/shard_map/ppermute | solution.py:144
  100.1 1.2 copy-start.6
  101.2 0.7 copy-start.9
  102.0 18.0 %all-to-all-start.4 = ((f32[4,2,2,64,384]{4,3,2,1,0:T(8,128)}), f32[4,2,2,64,384]{4,3,2,1,0:T(8,128)S(1)}, u32[]{:S(2)}, u32[]{:S(2)}) async-start(f32[4,2,2,64,384]{4,3,2,1,0:T(8,128)} %copy-done.6), calls=%async_computation.4 | async-start | bytes 3145728 | tf_op jit(solution)/shard_map/all_to_all | solution.py:152
  108.0 1.0 copy-start.8
  108.0 1.3 copy-start.10
  111.5 18.6 %copy-start.11 = (f32[4,1,1,64,384]{4,3,2,1,0:T(8,128)S(1)}, f32[4,1,1,64,384]{4,3,2,1,0:T(8,128)}, u32[]{:S(2)}) copy-start(f32[4,1,1,64,384]{4,3,2,1,0:T(8,128)} %get-tuple-element.11) | copy-start | bytes 1179652
  111.5 18.6 %collective-permute-start.4 = (f32[2,384,384]{2,1,0:T(8,128)}, f32[2,384,384]{2,1,0:T(8,128)}, u32[]{:S(2)}, u32[]{:S(2)}) collective-permute-start(f32[2,384,384]{2,1,0:T(8,128)} %pad_maximum_fusion), channel_id=1, source_target_pairs={{0,64},{64,0},{128,192},{192,128},{256,320},{320,256},{384,448},{4... | collective-permute-start | bytes 3538952 | tf_op jit(solution)/shard_map/ppermute | solution.py:148
  120.8 18.4 %all-to-all-start.5 = ((f32[16,2,8,384]{3,2,1,0:T(8,128)}), f32[16,2,8,384]{3,2,1,0:T(8,128)S(1)}, u32[]{:S(2)}, u32[]{:S(2)}) async-start(f32[16,2,8,384]{3,2,1,0:T(8,128)} %bitcast.5), calls=%async_computation.5 | async-start | bytes 786432 | tf_op jit(solution)/shard_map/all_to_all | solution.py:152

commit v6 on v5

--- a/solution.py
+++ b/solution.py
@@ -71,8 +71,8 @@
     return dot(left[0], right[0]) + (dot(left[0], right[1]) + dot(left[1], right[0]))
 
 
-def terms_kernel(first, share, inputs, expand, expand_far, reduce, reduce_far, out):
-    weights = ((expand, expand_far), (reduce, reduce_far))
+def terms_kernel(first, share, inputs, expand, expand_far, reduces, out):
+    weights = ((expand, expand_far), (reduces.at[0], reduces.at[1]))
     for array in range(2):
         total = None
         for pair in range(2):
@@ -85,13 +85,13 @@
             out[q, array] = total[q * share : (q + 1) * share]
 
 
-def results_kernel(earlier, both, expand, expand_far, reduce, reduce_far, out):
+def results_kernel(earlier, both, expand, expand_far, reduces, out):
     at = 0
     if earlier is not None:
         at = earlier.shape[0]
         out[:at] = earlier[...]
     rows = out.shape[3]
-    weights = ((reduce, reduce_far), (expand, expand_far))
+    weights = ((reduces.at[0], reduces.at[1]), (expand, expand_far))
     for array in range(2):
         block = halves(jnp.concatenate([both[q, array] for q in range(QUAD)], axis=0))
         for pair in range(2):
@@ -173,12 +173,12 @@
     inputs = exchange(inputs, CELL, BLOCKS)
 
     expand = (expand_weight, other_expand)
-    reduce = (reduce_weight, swap_pair(reduce_weight))
+    reduces = jnp.stack([reduce_weight, swap_pair(reduce_weight)])
 
     half = N_NEAR // 2 * rows
     share = half // QUAD
     flops = 3 * 2 * 4 * half * width * hidden
-    weights = (*expand, *reduce)
+    weights = (*expand, reduces)
 
     def terms(first):
         return local_call(

time: 141 us -> 143 us (1.014)
  Pallas kernels: 5.37 us -> 6.84 us
    all_to_all x4, waiting for transfers between devices: 12.8 us -> 15.4 us  [exchange(): lax.all_to_all(blocks, axis, split_axis=0, concat_axis=0, tiled=True, axi...]
    ppermute x3, waiting for transfers between devices: 20.9 us -> 19 us  [swap_pair(): return lax.ppermute(block, ('y', 'core'), PARTNERS)]
    pallas_call x6, Pallas kernels: 5.37 us -> 6.84 us  [local_call(): pl.pallas_call(kernel, out_shape=jax.ShapeDtypeStruct(shape, jnp.float32)...]
    unnamed x24 -> x22, local copies, waits for them, and re-layouts: 5.28 us -> 5.05 us
  transfers between devices with their start and end apart: 9 -> 9, of which waited for: 8 -> 8; matrix products, arithmetic and copies ran while one was open for 6% -> 6% of each run, Pallas kernels for 2% -> 3%
where the time goes in v6:
time: 143 us; the launch traced here: 142 us
  starting transfers between devices  53.1 us (37%)
  waiting for transfers between devices  35.2 us (25%)
  blocking collectives  29.4 us (21%)
  Pallas kernels  6.84 us (5%)
  local copies, waits for them, and re-layouts  6.67 us (5%)
  matrix products  5.84 us (4%)
  other arithmetic  4.18 us (3%)
    all_to_all x4, starting transfers between devices, exchange(): lax.all_to_all(blocks, axis, split_axis=0, concat_axis=0, tiled=True, axi...  31.4 us
    all_to_all x2, blocking collectives, exchange(): lax.all_to_all(blocks, axis, split_axis=0, concat_axis=0, tiled=True, axi...  29.4 us
    ppermute x3, waiting for transfers between devices, swap_pair(): return lax.ppermute(block, ('y', 'core'), PARTNERS)  19 us
    all_to_all x4, waiting for transfers between devices, exchange(): lax.all_to_all(blocks, axis, split_axis=0, concat_axis=0, tiled=True, axi...  15.4 us
    ppermute x3, starting transfers between devices, swap_pair(): return lax.ppermute(block, ('y', 'core'), PARTNERS)  12.6 us
    ppermute x2, starting transfers between devices, swap_cores(): return lax.ppermute(block, 'core', [(0, 1), (1, 0)])  9.01 us
    pallas_call x6, Pallas kernels, local_call(): pl.pallas_call(kernel, out_shape=jax.ShapeDtypeStruct(shape, jnp.float32)...  6.84 us
    dot_general x4, matrix products, product(): lax.dot_general(left, right, (dims, ((), ())), precision=precise, preferr...  5.84 us
  transfers between devices with their start and end apart: 9, of which 8 were waited for; matrix products, arithmetic and copies ran while one was open for 6% of the time, Pallas kernels for 3%

profile of v6, /device:TPU:1, one launch (start us, length us, event | category | flops | bytes accessed | tf_op | source)
XLA Modules:
  0.0 142.1 jit_solution(11138994941047372992)
XLA Ops:
  0.6 0.0 copy-start
  0.6 0.8 pad_maximum_fusion.9
  1.5 0.8 broadcast_in_dim.4
  2.2 16.3 %all-to-all-start = ((f32[16,2,8,384]{3,2,1,0:T(8,128)}), f32[16,2,8,384]{3,2,1,0:T(8,128)S(1)}, u32[]{:S(2)}, u32[]{:S(2)}) async-start(f32[16,2,8,384]{3,2,1,0:T(8,128)} %bitcast.3), calls=%async_computation | async-start | bytes 786432 | tf_op jit(solution)/shard_map/all_to_all | solution.py:152
  18.6 0.0 copy-done
  18.6 4.5 %collective-permute-start = (f32[384,384]{1,0:T(8,128)S(1)}, f32[384,384]{1,0:T(8,128)S(1)}, u32[]{:S(2)}, u32[]{:S(2)}) collective-permute-start(f32[384,384]{1,0:T(8,128)S(1)} %copy-done), channel_id=1, source_target_pairs={{0,64},{64,0},{128,192},{192,128},{256,320},{320,256},{384,448},{4... | collective-permute-start | bytes 1769480 | tf_op jit(solution)/shard_map/ppermute | solution.py:148
  23.1 7.9 %collective-permute-done.expand_far = f32[384,384]{1,0:T(8,128)S(1)} collective-permute-done((f32[384,384]{1,0:T(8,128)S(1)}, f32[384,384]{1,0:T(8,128)S(1)}, u32[]{:S(2)}, u32[]{:S(2)}) %collective-permute-start) | collective-permute-done | bytes 589856 | tf_op jit(solution)/shard_map/ppermute | solution.py:148
  31.0 2.6 %all-to-all-done = f32[16,2,8,384]{3,2,1,0:T(8,128)S(1)} async-done(((f32[16,2,8,384]{3,2,1,0:T(8,128)}), f32[16,2,8,384]{3,2,1,0:T(8,128)S(1)}, u32[]{:S(2)}, u32[]{:S(2)}) %all-to-all-start) | async-done | bytes 393248 | tf_op jit(solution)/shard_map/all_to_all | solution.py:152
  33.7 0.1 shard_map.75
  33.8 1.2 copy-done.4
  34.9 5.5 %all-to-all-start.1 = ((f32[4,2,2,64,384]{4,3,2,1,0:T(8,128)}), f32[4,2,2,64,384]{4,3,2,1,0:T(8,128)S(1)}, u32[]{:S(2)}, u32[]{:S(2)}) async-start(f32[4,2,2,64,384]{4,3,2,1,0:T(8,128)} %copy-done.4), calls=%async_computation.1 | async-start | bytes 3145728 | tf_op jit(solution)/shard_map/all_to_all | solution.py:152
  40.4 0.0 copy-done.10
  40.4 5.6 %collective-permute-start.1 = (f32[384,384]{1,0:T(8,128)S(1)}, f32[384,384]{1,0:T(8,128)S(1)}, u32[]{:S(2)}, u32[]{:S(2)}) collective-permute-start(f32[384,384]{1,0:T(8,128)S(1)} %copy-done.10), channel_id=1, source_target_pairs={{0,64},{64,0},{128,192},{192,128},{256,320},{320,256},{384,448},{4... | collective-permute-start | bytes 1769480 | tf_op jit(solution)/shard_map/ppermute | solution.py:148
  46.0 7.3 %collective-permute-done.1 = f32[384,384]{1,0:T(8,128)S(1)} collective-permute-done((f32[384,384]{1,0:T(8,128)S(1)}, f32[384,384]{1,0:T(8,128)S(1)}, u32[]{:S(2)}, u32[]{:S(2)}) %collective-permute-start.1) | collective-permute-done | bytes 589856 | tf_op jit(solution)/shard_map/ppermute | solution.py:148
  53.3 1.1 pad_maximum_fusion.reduces
  54.4 0.0 all-to-all-done.1.inputs
  54.4 0.0 copy-start.2
  54.4 1.1 copy-done.2
  55.5 1.1 shard_map.77
  56.6 1.9 %collective-permute-start.2 = (f32[4,2,32,384]{3,2,1,0:T(8,128)S(1)}, f32[4,2,32,384]{3,2,1,0:T(8,128)S(1)}, u32[]{:S(2)}, u32[]{:S(2)}) collective-permute-start(f32[4,2,32,384]{3,2,1,0:T(8,128)S(1)} %shard_map.77), channel_id=1, source_target_pairs={{0,32},{32,0},{1,33},{33,1},{2,34},{34,2},{3,35},{35,3},{4,36},{36... | collective-permute-start | bytes 1179656 | tf_op jit(solution)/shard_map/ppermute | solution.py:144
  58.5 1.1 shard_map.76
  59.6 0.6 collective-permute-done.2
  60.3 15.2 %all_to_all.30 = f32[4,2,32,384]{3,2,1,0:T(8,128)} all-to-all(f32[4,2,32,384]{3,2,1,0:T(8,128)S(1)} %add.26), channel_id=1, replica_groups={{0,128,256,384},{64,192,320,448},{1,129,257,385},{65,193,321,449},{2,13..., dimensions={0} | all-to-all | bytes 786432 | tf_op jit(solution)/shard_map/all_to_all | solution.py:152
  75.4 1.0 reduce_sum.18
  76.5 0.0 copy-start.3
  76.6 14.3 %all_to_all.31.both = f32[4,2,32,384]{3,2,1,0:T(8,128)S(1)} all-to-all(f32[4,2,32,384]{3,2,1,0:T(8,128)S(1)} %broadcast_in_dim.5), channel_id=1, replica_groups={{0,128,256,384},{64,192,320,448},{1,129,257,385},{65,193,321,449},{2,13..., dimensions={0} | all-to-all | bytes 786432 | tf_op jit(solution)/shard_map/all_to_all | solution.py:152
  90.8 7.1 %collective-permute-start.3 = (f32[4,2,32,384]{3,2,1,0:T(8,128)S(1)}, f32[4,2,32,384]{3,2,1,0:T(8,128)S(1)}, u32[]{:S(2)}, u32[]{:S(2)}) collective-permute-start(f32[4,2,32,384]{3,2,1,0:T(8,128)S(1)} %all_to_all.31.both), channel_id=1, source_target_pairs={{0,32},{32,0},{1,33},{33,1},{2,34},{34,2},{3,35},{35,3},{4,36},{36... | collective-permute-start | bytes 1179656 | tf_op jit(solution)/shard_map/ppermute | solution.py:144
  97.9 1.1 shard_map.78.earlier
  99.1 0.2 collective-permute-done.3.both
  99.3 1.2 shard_map.79
  100.5 1.1 copy-done.5
  101.6 0.7 copy-done.8
  102.3 6.1 %all-to-all-start.4 = ((f32[4,2,2,64,384]{4,3,2,1,0:T(8,128)}), f32[4,2,2,64,384]{4,3,2,1,0:T(8,128)}, u32[]{:S(2)}, u32[]{:S(2)}) async-start(f32[4,2,2,64,384]{4,3,2,1,0:T(8,128)} %copy-done.5), calls=%async_computation.4 | async-start | bytes 3145728 | tf_op jit(solution)/shard_map/all_to_all | solution.py:152
  108.4 0.1 fusion.9
  108.5 0.8 copy-done.7
  109.4 0.1 copy-done.9
  109.5 0.5 convolution_bitcast_fusion
  110.1 0.5 convolution_bitcast_fusion.1
  110.6 1.1 pad_maximum_fusion.1
  111.7 2.6 %collective-permute-start.4 = (f32[2,384,384]{2,1,0:T(8,128)}, f32[2,384,384]{2,1,0:T(8,128)}, u32[]{:S(2)}, u32[]{:S(2)}) collective-permute-start(f32[2,384,384]{2,1,0:T(8,128)} %pad_maximum_fusion.1), channel_id=1, source_target_pairs={{0,64},{64,0},{128,192},{192,128},{256,320},{320,256},{384,448},{4... | collective-permute-start | bytes 3538952 | tf_op jit(solution)/shard_map/ppermute | solution.py:148
  114.3 6.2 %all-to-all-done.4.near = f32[4,2,2,64,384]{4,3,2,1,0:T(8,128)} async-done(((f32[4,2,2,64,384]{4,3,2,1,0:T(8,128)}), f32[4,2,2,64,384]{4,3,2,1,0:T(8,128)}, u32[]{:S(2)}, u32[]{:S(2)}) %all-to-all-start.4) | async-done | bytes 1572896 | tf_op jit(solution)/shard_map/all_to_all | solution.py:152
  120.5 2.3 %shard_map.80 = f32[8,2,2,8,384]{4,3,2,1,0:T(8,128)} custom-call(s32[1]{0:T(128)} %bitcast.odd, f32[4,2,2,64,384]{4,3,2,1,0:T(8,128)} %all-to-all-done.4.near), custom_call_target="tpu_custom_call" | custom-call | flops 393216 | bytes 1966084 | tf_op jit(solution)/shard_map/pallas_call | solution.py:128
  122.7 3.6 %all-to-all-start.5 = ((f32[16,2,8,384]{3,2,1,0:T(8,128)}), f32[16,2,8,384]{3,2,1,0:T(8,128)S(1)}, u32[]{:S(2)}, u32[]{:S(2)}) async-start(f32[16,2,8,384]{3,2,1,0:T(8,128)} %bitcast.7), calls=%async_computation.5 | async-start | bytes 786432 | tf_op jit(solution)/shard_map/all_to_all | solution.py:152
  126.3 3.8 %collective-permute-done.4 = f32[2,384,384]{2,1,0:T(8,128)} collective-permute-done((f32[2,384,384]{2,1,0:T(8,128)}, f32[2,384,384]{2,1,0:T(8,128)}, u32[]{:S(2)}, u32[]{:S(2)}) %collective-permute-start.4) | collective-permute-done | bytes 1179680 | tf_op jit(solution)/shard_map/ppermute | solution.py:148
  130.1 2.4 %convolution_add_fusion.1 = f32[384,384]{1,0:T(8,128)} fusion(f32[256,384]{1,0:T(8,128)S(1)} %bitcast.50, f32[2,384,384]{2,1,0:T(8,128)} %collective-permute-done.4, f32[128,384]{1,0:T(8,128)S(1)} %bitcast.45, f32[128,384]{1,0:T(8,128)S(1)} %bitcast.43), kind=kOutput, calls=%fused_computation.3 | convolution fusion | flops 226738176 | bytes 1966080 | tf_op jit(solution)/shard_map/dot_general | solution.py:55
  132.5 2.4 %convolution_add_fusion = f32[384,384]{1,0:T(8,128)} fusion(f32[256,384]{1,0:T(8,128)S(1)} %bitcast.49, f32[2,384,384]{2,1,0:T(8,128)} %collective-permute-done.4, f32[128,384]{1,0:T(8,128)S(1)} %bitcast.41, f32[128,384]{1,0:T(8,128)S(1)} %bitcast.39), kind=kOutput, calls=%fused_computation | convolution fusion | flops 226738176 | bytes 1966080 | tf_op jit(solution)/shard_map/dot_general | solution.py:55
  134.9 6.5 %all-to-all-done.5 = f32[16,2,8,384]{3,2,1,0:T(8,128)S(1)} async-done(((f32[16,2,8,384]{3,2,1,0:T(8,128)}), f32[16,2,8,384]{3,2,1,0:T(8,128)S(1)}, u32[]{:S(2)}, u32[]{:S(2)}) %all-to-all-start.5) | async-done | bytes 393248 | tf_op jit(solution)/shard_map/all_to_all | solution.py:152
  141.5 0.6 slice_bitcast_fusion.2
  (19 shorter events, 0.2 us)
Async XLA Ops:
  0.6 17.9 %copy-start = (f32[384,384]{1,0:T(8,128)S(1)}, f32[384,384]{1,0:T(8,128)}, u32[]{:S(2)}) copy-start(f32[384,384]{1,0:T(8,128)} %expand.7) | copy-start | bytes 1769476
  2.2 31.4 %all-to-all-start = ((f32[16,2,8,384]{3,2,1,0:T(8,128)}), f32[16,2,8,384]{3,2,1,0:T(8,128)S(1)}, u32[]{:S(2)}, u32[]{:S(2)}) async-start(f32[16,2,8,384]{3,2,1,0:T(8,128)} %bitcast.3), calls=%async_computation | async-start | bytes 786432 | tf_op jit(solution)/shard_map/all_to_all | solution.py:152
  18.6 12.4 %collective-permute-start = (f32[384,384]{1,0:T(8,128)S(1)}, f32[384,384]{1,0:T(8,128)S(1)}, u32[]{:S(2)}, u32[]{:S(2)}) collective-permute-start(f32[384,384]{1,0:T(8,128)S(1)} %copy-done), channel_id=1, source_target_pairs={{0,64},{64,0},{128,192},{192,128},{256,320},{320,256},{384,448},{4... | collective-permute-start | bytes 1769480 | tf_op jit(solution)/shard_map/ppermute | solution.py:148
  31.0 3.9 %copy-start.1 = (f32[384,384]{1,0:T(8,128)}, f32[384,384]{1,0:T(8,128)S(1)}, u32[]{:S(2)}) copy-start(f32[384,384]{1,0:T(8,128)S(1)} %collective-permute-done.expand_far) | copy-start | bytes 1769476
  33.8 1.2 copy-start.4
  34.9 5.5 %copy-start.10 = (f32[384,384]{1,0:T(8,128)S(1)}, f32[384,384]{1,0:T(8,128)}, u32[]{:S(2)}) copy-start(f32[384,384]{1,0:T(8,128)} %param.7) | copy-start | bytes 1769476
  34.9 19.5 %all-to-all-start.1 = ((f32[4,2,2,64,384]{4,3,2,1,0:T(8,128)}), f32[4,2,2,64,384]{4,3,2,1,0:T(8,128)S(1)}, u32[]{:S(2)}, u32[]{:S(2)}) async-start(f32[4,2,2,64,384]{4,3,2,1,0:T(8,128)} %copy-done.4), calls=%async_computation.1 | async-start | bytes 3145728 | tf_op jit(solution)/shard_map/all_to_all | solution.py:152
  40.4 12.8 %collective-permute-start.1 = (f32[384,384]{1,0:T(8,128)S(1)}, f32[384,384]{1,0:T(8,128)S(1)}, u32[]{:S(2)}, u32[]{:S(2)}) collective-permute-start(f32[384,384]{1,0:T(8,128)S(1)} %copy-done.10), channel_id=1, source_target_pairs={{0,64},{64,0},{128,192},{192,128},{256,320},{320,256},{384,448},{4... | collective-permute-start | bytes 1769480 | tf_op jit(solution)/shard_map/ppermute | solution.py:148
  54.4 1.1 copy-start.2
  56.6 3.6 %collective-permute-start.2 = (f32[4,2,32,384]{3,2,1,0:T(8,128)S(1)}, f32[4,2,32,384]{3,2,1,0:T(8,128)S(1)}, u32[]{:S(2)}, u32[]{:S(2)}) collective-permute-start(f32[4,2,32,384]{3,2,1,0:T(8,128)S(1)} %shard_map.77), channel_id=1, source_target_pairs={{0,32},{32,0},{1,33},{33,1},{2,34},{34,2},{3,35},{35,3},{4,36},{36... | collective-permute-start | bytes 1179656 | tf_op jit(solution)/shard_map/ppermute | solution.py:144
  76.5 21.5 %copy-start.3 = (f32[384,384]{1,0:T(8,128)S(1)}, f32[384,384]{1,0:T(8,128)}, u32[]{:S(2)}) copy-start(f32[384,384]{1,0:T(8,128)} %copy-done.1) | copy-start | bytes 1769476
  90.8 8.2 %copy-start.6 = (f32[4,2,32,384]{3,2,1,0:T(8,128)}, f32[4,2,32,384]{3,2,1,0:T(8,128)S(1)}, u32[]{:S(2)}) copy-start(f32[4,2,32,384]{3,2,1,0:T(8,128)S(1)} %all_to_all.31.both) | copy-start | bytes 1179652
  90.8 8.4 %collective-permute-start.3 = (f32[4,2,32,384]{3,2,1,0:T(8,128)S(1)}, f32[4,2,32,384]{3,2,1,0:T(8,128)S(1)}, u32[]{:S(2)}, u32[]{:S(2)}) collective-permute-start(f32[4,2,32,384]{3,2,1,0:T(8,128)S(1)} %all_to_all.31.both), channel_id=1, source_target_pairs={{0,32},{32,0},{1,33},{33,1},{2,34},{34,2},{3,35},{35,3},{4,36},{36... | collective-permute-start | bytes 1179656 | tf_op jit(solution)/shard_map/ppermute | solution.py:144
  100.4 1.1 copy-start.5
  101.6 0.7 copy-start.8
  102.3 18.1 %all-to-all-start.4 = ((f32[4,2,2,64,384]{4,3,2,1,0:T(8,128)}), f32[4,2,2,64,384]{4,3,2,1,0:T(8,128)}, u32[]{:S(2)}, u32[]{:S(2)}) async-start(f32[4,2,2,64,384]{4,3,2,1,0:T(8,128)} %copy-done.5), calls=%async_computation.4 | async-start | bytes 3145728 | tf_op jit(solution)/shard_map/all_to_all | solution.py:152
  108.4 1.0 copy-start.7
  108.4 1.1 copy-start.9
  111.7 18.5 %collective-permute-start.4 = (f32[2,384,384]{2,1,0:T(8,128)}, f32[2,384,384]{2,1,0:T(8,128)}, u32[]{:S(2)}, u32[]{:S(2)}) collective-permute-start(f32[2,384,384]{2,1,0:T(8,128)} %pad_maximum_fusion.1), channel_id=1, source_target_pairs={{0,64},{64,0},{128,192},{192,128},{256,320},{320,256},{384,448},{4... | collective-permute-start | bytes 3538952 | tf_op jit(solution)/shard_map/ppermute | solution.py:148
  122.7 18.7 %all-to-all-start.5 = ((f32[16,2,8,384]{3,2,1,0:T(8,128)}), f32[16,2,8,384]{3,2,1,0:T(8,128)S(1)}, u32[]{:S(2)}, u32[]{:S(2)}) async-start(f32[16,2,8,384]{3,2,1,0:T(8,128)} %bitcast.7), calls=%async_computation.5 | async-start | bytes 786432 | tf_op jit(solution)/shard_map/all_to_all | solution.py:152

commit v7 on v5

--- a/solution.py
+++ b/solution.py
@@ -201,10 +201,18 @@
     other = swap_cores(own)
 
     tail = (2, 2, rows, width)
-    outs = local_call(
-        functools.partial(results_kernel, None), (N_NEAR // 2, *tail), flops, own, *weights
-    )
-    outs = local_call(results_kernel, (N_NEAR, *tail), flops, outs, other, *weights)
+    outs = jnp.concatenate(
+        [
+            local_call(
+                functools.partial(results_kernel, None),
+                (N_NEAR // 2, *tail),
+                flops,
+                both,
+                *weights,
+            )
+            for both in (own, other)
+        ]
+    )
     near = exchange(outs, CELL, BLOCKS)
     near = local_call(fold_kernel, (N_FAR, 2, 2, part, width), near.size, odd, near)
 

time: 141 us -> 141 us (level)
    unnamed x24 -> x22, local copies, waits for them, and re-layouts: 5.28 us -> 4.13 us
where the time goes in v7:
time: 141 us; the launch traced here: 140 us
  starting transfers between devices  53.4 us (38%)
  waiting for transfers between devices  34.5 us (24%)
  blocking collectives  29.4 us (21%)
  local copies, waits for them, and re-layouts  6.5 us (5%)
  matrix products  5.83 us (4%)
  Pallas kernels  5.3 us (4%)
  other arithmetic  4.27 us (3%)
    all_to_all x4, starting transfers between devices, exchange(): lax.all_to_all(blocks, axis, split_axis=0, concat_axis=0, tiled=True, axi...  31.6 us
    all_to_all x2, blocking collectives, exchange(): lax.all_to_all(blocks, axis, split_axis=0, concat_axis=0, tiled=True, axi...  29.4 us
    ppermute x3, waiting for transfers between devices, swap_pair(): return lax.ppermute(block, ('y', 'core'), PARTNERS)  20.7 us
    all_to_all x4, waiting for transfers between devices, exchange(): lax.all_to_all(blocks, axis, split_axis=0, concat_axis=0, tiled=True, axi...  13 us
    ppermute x3, starting transfers between devices, swap_pair(): return lax.ppermute(block, ('y', 'core'), PARTNERS)  12.8 us
    ppermute x2, starting transfers between devices, swap_cores(): return lax.ppermute(block, 'core', [(0, 1), (1, 0)])  9.01 us
    dot_general x4, matrix products, product(): lax.dot_general(left, right, (dims, ((), ())), precision=precise, preferr...  5.83 us
    pallas_call x6, Pallas kernels, local_call(): pl.pallas_call(kernel, out_shape=jax.ShapeDtypeStruct(shape, jnp.float32)...  5.3 us
  transfers between devices with their start and end apart: 9, of which 8 were waited for; matrix products, arithmetic and copies ran while one was open for 6% of the time, Pallas kernels for 2%

profile of v7, /device:TPU:1, one launch (start us, length us, event | category | flops | bytes accessed | tf_op | source)
XLA Modules:
  0.0 140.0 jit_solution(7369104693957094837)
XLA Ops:
  0.6 0.8 pad_maximum_fusion.9
  1.4 0.8 broadcast_in_dim.4
  2.2 16.3 %all-to-all-start = ((f32[16,2,8,384]{3,2,1,0:T(8,128)}), f32[16,2,8,384]{3,2,1,0:T(8,128)S(1)}, u32[]{:S(2)}, u32[]{:S(2)}) async-start(f32[16,2,8,384]{3,2,1,0:T(8,128)} %bitcast.3), calls=%async_computation | async-start | bytes 786432 | tf_op jit(solution)/shard_map/all_to_all | solution.py:152
  18.5 4.5 %collective-permute-start = (f32[384,384]{1,0:T(8,128)}, f32[384,384]{1,0:T(8,128)S(1)}, u32[]{:S(2)}, u32[]{:S(2)}) collective-permute-start(f32[384,384]{1,0:T(8,128)} %expand.7), channel_id=1, source_target_pairs={{0,64},{64,0},{128,192},{192,128},{256,320},{320,256},{384,448},{4... | collective-permute-start | bytes 1769480 | tf_op jit(solution)/shard_map/ppermute | solution.py:148
  23.0 8.0 %collective-permute-done.expand_far = f32[384,384]{1,0:T(8,128)S(1)} collective-permute-done((f32[384,384]{1,0:T(8,128)}, f32[384,384]{1,0:T(8,128)S(1)}, u32[]{:S(2)}, u32[]{:S(2)}) %collective-permute-start) | collective-permute-done | bytes 589856 | tf_op jit(solution)/shard_map/ppermute | solution.py:148
  31.0 2.6 %all-to-all-done = f32[16,2,8,384]{3,2,1,0:T(8,128)S(1)} async-done(((f32[16,2,8,384]{3,2,1,0:T(8,128)}), f32[16,2,8,384]{3,2,1,0:T(8,128)S(1)}, u32[]{:S(2)}, u32[]{:S(2)}) %all-to-all-start) | async-done | bytes 393248 | tf_op jit(solution)/shard_map/all_to_all | solution.py:152
  33.6 0.1 shard_map.75
  33.7 0.0 copy-start.5
  33.7 1.2 copy-done.5
  34.9 5.5 %all-to-all-start.1 = ((f32[4,2,2,64,384]{4,3,2,1,0:T(8,128)}), f32[4,2,2,64,384]{4,3,2,1,0:T(8,128)S(1)}, u32[]{:S(2)}, u32[]{:S(2)}) async-start(f32[4,2,2,64,384]{4,3,2,1,0:T(8,128)} %copy-done.5), calls=%async_computation.1 | async-start | bytes 3145728 | tf_op jit(solution)/shard_map/all_to_all | solution.py:152
  40.4 0.0 copy-done.1
  40.4 5.6 %collective-permute-start.1 = (f32[384,384]{1,0:T(8,128)S(1)}, f32[384,384]{1,0:T(8,128)S(1)}, u32[]{:S(2)}, u32[]{:S(2)}) collective-permute-start(f32[384,384]{1,0:T(8,128)S(1)} %copy-done.1), channel_id=1, source_target_pairs={{0,64},{64,0},{128,192},{192,128},{256,320},{320,256},{384,448},{4... | collective-permute-start | bytes 1769480 | tf_op jit(solution)/shard_map/ppermute | solution.py:148
  45.9 7.3 %collective-permute-done.1.reduce_far = f32[384,384]{1,0:T(8,128)S(1)} collective-permute-done((f32[384,384]{1,0:T(8,128)S(1)}, f32[384,384]{1,0:T(8,128)S(1)}, u32[]{:S(2)}, u32[]{:S(2)}) %collective-permute-start.1) | collective-permute-done | bytes 589856 | tf_op jit(solution)/shard_map/ppermute | solution.py:148
  53.2 0.8 copy-done.2
  54.0 0.0 all-to-all-done.1.inputs
  54.0 0.0 copy-done
  54.0 1.1 copy-done.3
  55.1 1.1 shard_map.77
  56.2 1.9 %collective-permute-start.2 = (f32[4,2,32,384]{3,2,1,0:T(8,128)S(1)}, f32[4,2,32,384]{3,2,1,0:T(8,128)S(1)}, u32[]{:S(2)}, u32[]{:S(2)}) collective-permute-start(f32[4,2,32,384]{3,2,1,0:T(8,128)S(1)} %shard_map.77), channel_id=1, source_target_pairs={{0,32},{32,0},{1,33},{33,1},{2,34},{34,2},{3,35},{35,3},{4,36},{36... | collective-permute-start | bytes 1179656 | tf_op jit(solution)/shard_map/ppermute | solution.py:144
  58.1 1.1 shard_map.76
  59.2 0.6 collective-permute-done.2
  59.9 15.2 %all_to_all.30 = f32[4,2,32,384]{3,2,1,0:T(8,128)} all-to-all(f32[4,2,32,384]{3,2,1,0:T(8,128)S(1)} %add.26), channel_id=1, replica_groups={{0,128,256,384},{64,192,320,448},{1,129,257,385},{65,193,321,449},{2,13..., dimensions={0} | all-to-all | bytes 786432 | tf_op jit(solution)/shard_map/all_to_all | solution.py:152
  75.0 1.0 reduce_sum.18
  76.1 0.0 copy-start.4
  76.2 14.3 %all_to_all.31.both = f32[4,2,32,384]{3,2,1,0:T(8,128)S(1)} all-to-all(f32[4,2,32,384]{3,2,1,0:T(8,128)S(1)} %broadcast_in_dim.5), channel_id=1, replica_groups={{0,128,256,384},{64,192,320,448},{1,129,257,385},{65,193,321,449},{2,13..., dimensions={0} | all-to-all | bytes 786432 | tf_op jit(solution)/shard_map/all_to_all | solution.py:152
  90.4 7.1 %collective-permute-start.3 = (f32[4,2,32,384]{3,2,1,0:T(8,128)S(1)}, f32[4,2,32,384]{3,2,1,0:T(8,128)S(1)}, u32[]{:S(2)}, u32[]{:S(2)}) collective-permute-start(f32[4,2,32,384]{3,2,1,0:T(8,128)S(1)} %all_to_all.31.both), channel_id=1, source_target_pairs={{0,32},{32,0},{1,33},{33,1},{2,34},{34,2},{3,35},{35,3},{4,36},{36... | collective-permute-start | bytes 1179656 | tf_op jit(solution)/shard_map/ppermute | solution.py:144
  97.5 1.1 shard_map.78
  98.7 0.2 collective-permute-done.3.both
  98.9 1.1 shard_map.79
  100.0 0.0 copy-start.8
  100.0 0.7 copy-done.8
  100.7 1.3 pad_maximum_fusion
  102.0 6.1 %all-to-all-start.4 = ((f32[4,2,2,64,384]{4,3,2,1,0:T(8,128)}), f32[4,2,2,64,384]{4,3,2,1,0:T(8,128)S(1)}, u32[]{:S(2)}, u32[]{:S(2)}) async-start(f32[4,2,2,64,384]{4,3,2,1,0:T(8,128)} %pad_maximum_fusion), calls=%async_computation.4 | async-start | bytes 3145728 | tf_op jit(solution)/shard_map/all_to_all | solution.py:152
  108.0 0.9 fusion.9
  108.9 0.1 copy-done.7
  109.1 0.2 copy-done.9
  109.3 0.5 convolution_bitcast_fusion
  109.8 0.5 convolution_bitcast_fusion.1
  110.4 1.1 pad_maximum_fusion.1
  111.5 2.7 %collective-permute-start.4 = (f32[2,384,384]{2,1,0:T(8,128)}, f32[2,384,384]{2,1,0:T(8,128)}, u32[]{:S(2)}, u32[]{:S(2)}) collective-permute-start(f32[2,384,384]{2,1,0:T(8,128)} %pad_maximum_fusion.1), channel_id=1, source_target_pairs={{0,64},{64,0},{128,192},{192,128},{256,320},{320,256},{384,448},{4... | collective-permute-start | bytes 3538952 | tf_op jit(solution)/shard_map/ppermute | solution.py:148
  114.2 5.8 %all-to-all-done.4.near = f32[4,2,2,64,384]{4,3,2,1,0:T(8,128)S(1)} async-done(((f32[4,2,2,64,384]{4,3,2,1,0:T(8,128)}), f32[4,2,2,64,384]{4,3,2,1,0:T(8,128)S(1)}, u32[]{:S(2)}, u32[]{:S(2)}) %all-to-all-start.4) | async-done | bytes 1572896 | tf_op jit(solution)/shard_map/all_to_all | solution.py:152
  120.0 0.8 shard_map.80
  120.8 3.8 %all-to-all-start.5 = ((f32[16,2,8,384]{3,2,1,0:T(8,128)}), f32[16,2,8,384]{3,2,1,0:T(8,128)S(1)}, u32[]{:S(2)}, u32[]{:S(2)}) async-start(f32[16,2,8,384]{3,2,1,0:T(8,128)} %bitcast.5), calls=%async_computation.5 | async-start | bytes 786432 | tf_op jit(solution)/shard_map/all_to_all | solution.py:152
  124.6 5.5 %collective-permute-done.4 = f32[2,384,384]{2,1,0:T(8,128)} collective-permute-done((f32[2,384,384]{2,1,0:T(8,128)}, f32[2,384,384]{2,1,0:T(8,128)}, u32[]{:S(2)}, u32[]{:S(2)}) %collective-permute-start.4) | collective-permute-done | bytes 1179680 | tf_op jit(solution)/shard_map/ppermute | solution.py:148
  130.1 2.4 %convolution_add_fusion.1 = f32[384,384]{1,0:T(8,128)} fusion(f32[256,384]{1,0:T(8,128)S(1)} %bitcast.48, f32[2,384,384]{2,1,0:T(8,128)} %collective-permute-done.4, f32[128,384]{1,0:T(8,128)S(1)} %bitcast.43, f32[128,384]{1,0:T(8,128)S(1)} %bitcast.41), kind=kOutput, calls=%fused_computation.4 | convolution fusion | flops 226738176 | bytes 1966080 | tf_op jit(solution)/shard_map/dot_general | solution.py:55
  132.5 2.4 %convolution_add_fusion = f32[384,384]{1,0:T(8,128)} fusion(f32[256,384]{1,0:T(8,128)S(1)} %bitcast.47, f32[2,384,384]{2,1,0:T(8,128)} %collective-permute-done.4, f32[128,384]{1,0:T(8,128)S(1)} %bitcast.39, f32[128,384]{1,0:T(8,128)S(1)} %bitcast.37), kind=kOutput, calls=%fused_computation.1 | convolution fusion | flops 226738176 | bytes 1966080 | tf_op jit(solution)/shard_map/dot_general | solution.py:55
  134.9 4.5 %all-to-all-done.5 = f32[16,2,8,384]{3,2,1,0:T(8,128)S(1)} async-done(((f32[16,2,8,384]{3,2,1,0:T(8,128)}), f32[16,2,8,384]{3,2,1,0:T(8,128)S(1)}, u32[]{:S(2)}, u32[]{:S(2)}) %all-to-all-start.5) | async-done | bytes 393248 | tf_op jit(solution)/shard_map/all_to_all | solution.py:152
  139.4 0.6 slice_bitcast_fusion.2
  (19 shorter events, 0.2 us)
Async XLA Ops:
  2.2 31.4 %all-to-all-start = ((f32[16,2,8,384]{3,2,1,0:T(8,128)}), f32[16,2,8,384]{3,2,1,0:T(8,128)S(1)}, u32[]{:S(2)}, u32[]{:S(2)}) async-start(f32[16,2,8,384]{3,2,1,0:T(8,128)} %bitcast.3), calls=%async_computation | async-start | bytes 786432 | tf_op jit(solution)/shard_map/all_to_all | solution.py:152
  18.5 12.5 %collective-permute-start = (f32[384,384]{1,0:T(8,128)}, f32[384,384]{1,0:T(8,128)S(1)}, u32[]{:S(2)}, u32[]{:S(2)}) collective-permute-start(f32[384,384]{1,0:T(8,128)} %expand.7), channel_id=1, source_target_pairs={{0,64},{64,0},{128,192},{192,128},{256,320},{320,256},{384,448},{4... | collective-permute-start | bytes 1769480 | tf_op jit(solution)/shard_map/ppermute | solution.py:148
  33.7 1.2 copy-start.5
  34.9 5.5 %copy-start.1 = (f32[384,384]{1,0:T(8,128)S(1)}, f32[384,384]{1,0:T(8,128)}, u32[]{:S(2)}) copy-start(f32[384,384]{1,0:T(8,128)} %reduce.7) | copy-start | bytes 1769476
  34.9 19.2 %copy-start = (f32[384,384]{1,0:T(8,128)S(1)}, f32[384,384]{1,0:T(8,128)}, u32[]{:S(2)}) copy-start(f32[384,384]{1,0:T(8,128)} %expand.7) | copy-start | bytes 1769476
  34.9 19.2 %all-to-all-start.1 = ((f32[4,2,2,64,384]{4,3,2,1,0:T(8,128)}), f32[4,2,2,64,384]{4,3,2,1,0:T(8,128)S(1)}, u32[]{:S(2)}, u32[]{:S(2)}) async-start(f32[4,2,2,64,384]{4,3,2,1,0:T(8,128)} %copy-done.5), calls=%async_computation.1 | async-start | bytes 3145728 | tf_op jit(solution)/shard_map/all_to_all | solution.py:152
  40.4 12.8 %collective-permute-start.1 = (f32[384,384]{1,0:T(8,128)S(1)}, f32[384,384]{1,0:T(8,128)S(1)}, u32[]{:S(2)}, u32[]{:S(2)}) collective-permute-start(f32[384,384]{1,0:T(8,128)S(1)} %copy-done.1), channel_id=1, source_target_pairs={{0,64},{64,0},{128,192},{192,128},{256,320},{320,256},{384,448},{4... | collective-permute-start | bytes 1769480 | tf_op jit(solution)/shard_map/ppermute | solution.py:148
  53.2 0.8 copy-start.2
  54.0 1.1 copy-start.3
  56.2 3.6 %collective-permute-start.2 = (f32[4,2,32,384]{3,2,1,0:T(8,128)S(1)}, f32[4,2,32,384]{3,2,1,0:T(8,128)S(1)}, u32[]{:S(2)}, u32[]{:S(2)}) collective-permute-start(f32[4,2,32,384]{3,2,1,0:T(8,128)S(1)} %shard_map.77), channel_id=1, source_target_pairs={{0,32},{32,0},{1,33},{33,1},{2,34},{34,2},{3,35},{35,3},{4,36},{36... | collective-permute-start | bytes 1179656 | tf_op jit(solution)/shard_map/ppermute | solution.py:144
  76.1 21.5 %copy-start.4 = (f32[384,384]{1,0:T(8,128)S(1)}, f32[384,384]{1,0:T(8,128)}, u32[]{:S(2)}) copy-start(f32[384,384]{1,0:T(8,128)} %copy-done.2) | copy-start | bytes 1769476
  90.4 8.2 %copy-start.6 = (f32[4,2,32,384]{3,2,1,0:T(8,128)}, f32[4,2,32,384]{3,2,1,0:T(8,128)S(1)}, u32[]{:S(2)}) copy-start(f32[4,2,32,384]{3,2,1,0:T(8,128)S(1)} %all_to_all.31.both) | copy-start | bytes 1179652
  90.4 8.4 %collective-permute-start.3 = (f32[4,2,32,384]{3,2,1,0:T(8,128)S(1)}, f32[4,2,32,384]{3,2,1,0:T(8,128)S(1)}, u32[]{:S(2)}, u32[]{:S(2)}) collective-permute-start(f32[4,2,32,384]{3,2,1,0:T(8,128)S(1)} %all_to_all.31.both), channel_id=1, source_target_pairs={{0,32},{32,0},{1,33},{33,1},{2,34},{34,2},{3,35},{35,3},{4,36},{36... | collective-permute-start | bytes 1179656 | tf_op jit(solution)/shard_map/ppermute | solution.py:144
  100.0 0.7 copy-start.8
  102.0 18.0 %all-to-all-start.4 = ((f32[4,2,2,64,384]{4,3,2,1,0:T(8,128)}), f32[4,2,2,64,384]{4,3,2,1,0:T(8,128)S(1)}, u32[]{:S(2)}, u32[]{:S(2)}) async-start(f32[4,2,2,64,384]{4,3,2,1,0:T(8,128)} %pad_maximum_fusion), calls=%async_computation.4 | async-start | bytes 3145728 | tf_op jit(solution)/shard_map/all_to_all | solution.py:152
  108.0 1.0 copy-start.7
  108.0 1.3 copy-start.9
  111.5 18.6 %copy-start.10 = (f32[4,1,1,64,384]{4,3,2,1,0:T(8,128)S(1)}, f32[4,1,1,64,384]{4,3,2,1,0:T(8,128)}, u32[]{:S(2)}) copy-start(f32[4,1,1,64,384]{4,3,2,1,0:T(8,128)} %get-tuple-element.11) | copy-start | bytes 1179652
  111.5 18.6 %collective-permute-start.4 = (f32[2,384,384]{2,1,0:T(8,128)}, f32[2,384,384]{2,1,0:T(8,128)}, u32[]{:S(2)}, u32[]{:S(2)}) collective-permute-start(f32[2,384,384]{2,1,0:T(8,128)} %pad_maximum_fusion.1), channel_id=1, source_target_pairs={{0,64},{64,0},{128,192},{192,128},{256,320},{320,256},{384,448},{4... | collective-permute-start | bytes 3538952 | tf_op jit(solution)/shard_map/ppermute | solution.py:148
  120.8 18.6 %all-to-all-start.5 = ((f32[16,2,8,384]{3,2,1,0:T(8,128)}), f32[16,2,8,384]{3,2,1,0:T(8,128)S(1)}, u32[]{:S(2)}, u32[]{:S(2)}) async-start(f32[16,2,8,384]{3,2,1,0:T(8,128)} %bitcast.5), calls=%async_computation.5 | async-start | bytes 786432 | tf_op jit(solution)/shard_map/all_to_all | solution.py:152
